TPU v7x, 128 devices: a whole 4x4x4 slice. The times are simulated.
128 devices in a mesh: batch: 8 (over x, core), proto: 16 (over y, z).
Axes of the slice: x: 4, y: 4, z: 4, core: 2. Of those that a mesh axis runs over, the one named last changes fastest.
Arguments:
- student_feats: bfloat16 [4096, 384], P('batch'), may hold values from -6 to 6
- teacher_feats: bfloat16 [4096, 384], P('batch'), may hold values from -9 to 9
- student_protos: bfloat16 [131072, 384], P('proto'), may hold values from -1 to 1
- teacher_protos: bfloat16 [131072, 384], P('proto'), may hold values from -9 to 9
Outputs:
- grad_proto: bfloat16 [131072, 384], P('proto')
- grad_student: bfloat16 [4096, 384], P('batch')
All inputs are finite; a program needn't handle non-finite values.
Results may differ from a plain program's by a relative error of at most 0.0076.
Values may be sent and summed in bfloat16 or wider, within the bound.
A program may use at most 128 MiB of HBM per device.

v0:
```python
import jax
import jax.numpy as jnp
from jax import lax
from jax.sharding import PartitionSpec as P

ITERS = 3


eps = 1e-06
teacher_temp = 0.04
student_temp = 0.1


def unit_rows(matrix):
    values = matrix.astype(jnp.float32)
    scale = lax.rsqrt(jnp.sum(values * values, axis=1, keepdims=True) + eps)
    return (values * scale, scale)


def similar(left, right):
    return lax.dot_general(
        left, right, (((1,), (1,)), ((), ())), preferred_element_type=jnp.float32
    )


def back_norm(grad, unit, scale):
    return scale * (grad - unit * jnp.sum(grad * unit, axis=1, keepdims=True))


def on_device(student_feats, teacher_feats, student_protos, teacher_protos):
    stud_float, stud_scale = unit_rows(student_feats)
    teach_float, teach_scale = unit_rows(teacher_feats)
    proto_float, proto_scale = unit_rows(student_protos)
    anchor_float, anchor_scale = unit_rows(teacher_protos)
    stud_unit = stud_float.astype(jnp.bfloat16)
    teach_unit = teach_float.astype(jnp.bfloat16)
    proto_unit = proto_float.astype(jnp.bfloat16)
    anchor_unit = anchor_float.astype(jnp.bfloat16)
    tok_local = student_feats.shape[0]
    proto_local = student_protos.shape[0]
    tok_all = tok_local * lax.axis_size("batch")
    proto_all = proto_local * lax.axis_size("proto")
    teach_exp = jnp.exp(similar(teach_unit, anchor_unit) / teacher_temp)
    row_weight = jnp.ones((tok_local,), jnp.float32)
    col_weight = jnp.ones((proto_local,), jnp.float32)
    for sweep in range(ITERS):
        col_part = jnp.sum(teach_exp * row_weight[:, None], axis=0)
        col_weight = 1.0 / (proto_all * lax.psum(col_part, "batch"))
        row_part = jnp.sum(teach_exp * col_weight[None, :], axis=1)
        row_weight = 1.0 / (tok_all * lax.psum(row_part, "proto"))
    targets = tok_all * teach_exp * row_weight[:, None] * col_weight[None, :]
    logits = similar(stud_unit, proto_unit) / student_temp
    exp_logits = jnp.exp(logits)
    total = lax.psum(jnp.sum(exp_logits, axis=1), "proto")
    delta = ((exp_logits / total[:, None] - targets) / (student_temp * tok_all)).astype(
        jnp.bfloat16
    )
    proto_back = lax.dot_general(
        delta, stud_unit, (((0,), (0,)), ((), ())), preferred_element_type=jnp.float32
    )
    proto_back = lax.psum(proto_back, "batch")
    grad_proto = back_norm(proto_back, proto_float, proto_scale).astype(jnp.bfloat16)
    feat_back = jnp.dot(delta, proto_unit, preferred_element_type=jnp.float32)
    feat_back = lax.psum(feat_back, "proto")
    grad_student = back_norm(feat_back, stud_float, stud_scale).astype(jnp.bfloat16)
    return (grad_proto, grad_student)


def solution(mesh):
    in_specs = (P("batch", None), P("batch", None), P("proto", None), P("proto", None))
    out_specs = (P("proto", None), P("batch", None))
    return jax.shard_map(
        on_device, mesh=mesh, in_specs=in_specs, out_specs=out_specs, check_vma=False
    )
```

profile of v0, /device:TPU:0, one launch (start us, length us, event | category | flops | bytes accessed | tf_op | source)
XLA Modules:
  0.0 533.1 jit_solution(3080825116178172458)
XLA Ops:
  7.2 0.0 all-reduce.6.cloned.1.call-start
  7.2 1.3 fusion.25
  8.5 1.1 fusion.24
  9.7 4.3 fusion.9
  14.0 4.1 fusion.8
  18.2 8.1 %fusion.32 = (f32[8192]{0:T(1024)S(1)}, f32[512,8192]{1,0:T(8,128)}) fusion(bf16[8192,384]{1,0:T(8,128)(2,1)S(1)} %bitcast.5, f32[8192]{0:T(1024)S(1)} %add_rsqrt_fusion, bf16[512,384]{1,0:T(8,128)(2,1)S(1)} %copy-done.3, f32[512]{0:T(512)S(1)} %add_rsqrt_fusion.2), kind=kOutput, calls=%fused_computation.52 | convolution fusion | flops 3239632896 | bytes 23529472 | tf_op jit(solution)/shard_map/dot_general | solution.py:21
  26.2 25.7 %psum.64 = f32[8192]{0:T(1024)S(1)} all-reduce(f32[8192]{0:T(1024)S(1)} %get-tuple-element.4), channel_id=1, replica_groups=mesh['batch'=8,'proto'=16] {'batch'}, use_global_device_ids=true, to_apply=%region_7.0 | all-reduce | flops 8192 | bytes 65536 | tf_op jit(solution)/shard_map/psum | solution.py:48
  52.0 7.3 %multiply_reduce_fusion.4 = f32[512]{0:T(512)S(1)} fusion(f32[512,8192]{1,0:T(8,128)} %get-tuple-element.5, f32[8192]{0:T(1024)S(1)} %multiply_divide_fusion.2), kind=kLoop, calls=%fused_computation.5 | loop fusion | flops 8388096 | bytes 16812032 | tf_op jit(solution)/shard_map/reduce_sum | solution.py:49
  59.2 41.9 %psum.65 = f32[512]{0:T(512)S(1)} all-reduce(f32[512]{0:T(512)S(1)} %multiply_reduce_fusion.4), channel_id=1, replica_groups=mesh['batch'=8,'proto'=16] {'proto'}, use_global_device_ids=true, to_apply=%region_9.0 | all-reduce | flops 512 | bytes 4096 | tf_op jit(solution)/shard_map/psum | solution.py:50
  101.2 8.3 %multiply_reduce_fusion.3 = f32[8192]{0:T(1024)S(1)} fusion(f32[512,8192]{1,0:T(8,128)} %get-tuple-element.5, f32[512]{0:T(512)S(1)} %multiply_divide_fusion.4), kind=kLoop, calls=%fused_computation.4 | loop fusion | flops 8380416 | bytes 16812032 | tf_op jit(solution)/shard_map/reduce_sum | solution.py:47
  109.5 23.6 %psum.66 = f32[8192]{0:T(1024)S(1)} all-reduce(f32[8192]{0:T(1024)S(1)} %multiply_reduce_fusion.3), channel_id=1, replica_groups=mesh['batch'=8,'proto'=16] {'batch'}, use_global_device_ids=true, to_apply=%region_11.0 | all-reduce | flops 8192 | bytes 65536 | tf_op jit(solution)/shard_map/psum | solution.py:48
  133.1 7.3 %multiply_reduce_fusion.2 = f32[512]{0:T(512)S(1)} fusion(f32[512,8192]{1,0:T(8,128)} %get-tuple-element.5, f32[8192]{0:T(1024)S(1)} %multiply_divide_fusion.1), kind=kLoop, calls=%fused_computation.3 | loop fusion | flops 8388096 | bytes 16812032 | tf_op jit(solution)/shard_map/reduce_sum | solution.py:49
  140.4 35.6 %psum.67 = f32[512]{0:T(512)S(1)} all-reduce(f32[512]{0:T(512)S(1)} %multiply_reduce_fusion.2), channel_id=1, replica_groups=mesh['batch'=8,'proto'=16] {'proto'}, use_global_device_ids=true, to_apply=%region_13.0 | all-reduce | flops 512 | bytes 4096 | tf_op jit(solution)/shard_map/psum | solution.py:50
  176.0 8.3 %multiply_reduce_fusion.1 = f32[8192]{0:T(1024)S(1)} fusion(f32[512,8192]{1,0:T(8,128)} %get-tuple-element.5, f32[512]{0:T(512)S(1)} %multiply_divide_fusion.3), kind=kLoop, calls=%fused_computation.2 | loop fusion | flops 8380416 | bytes 16812032 | tf_op jit(solution)/shard_map/reduce_sum | solution.py:47
  184.3 23.7 %psum.68 = f32[8192]{0:T(1024)S(1)} all-reduce(f32[8192]{0:T(1024)S(1)} %multiply_reduce_fusion.1), channel_id=1, replica_groups=mesh['batch'=8,'proto'=16] {'batch'}, use_global_device_ids=true, to_apply=%region_15.0 | all-reduce | flops 8192 | bytes 65536 | tf_op jit(solution)/shard_map/psum | solution.py:48
  208.1 7.0 %multiply_reduce_fusion = f32[512]{0:T(512)S(1)} fusion(f32[512,8192]{1,0:T(8,128)} %get-tuple-element.5, f32[8192]{0:T(1024)S(1)} %multiply_divide_fusion), kind=kLoop, calls=%fused_computation.1 | loop fusion | flops 8388096 | bytes 16812032 | tf_op jit(solution)/shard_map/reduce_sum | solution.py:49
  215.1 10.4 %fusion.3 = (f32[512]{0:T(512)S(1)}, f32[512,8192]{1,0:T(8,128)}) fusion(bf16[8192,384]{1,0:T(8,128)(2,1)} %param.6, f32[8192]{0:T(1024)S(1)} %add_rsqrt_fusion.1, bf16[512,384]{1,0:T(8,128)(2,1)S(1)} %copy-done.2, f32[512]{0:T(512)S(1)} %add_rsqrt_fusion.3), kind=kOutput, calls=%fused_computation.15 | convolution fusion | flops 3239640576 | bytes 23498752 | tf_op jit(solution)/shard_map/dot_general | solution.py:21
  225.5 37.4 %all-reduce = (f32[512]{0:T(512)S(1)}, f32[512]{0:T(512)S(1)}) all-reduce(f32[512]{0:T(512)S(1)} %multiply_reduce_fusion, f32[512]{0:T(512)S(1)} %get-tuple-element.6), channel_id=1, replica_groups=mesh['batch'=8,'proto'=16] {'proto'}, use_global_device_ids=true, to_apply=%region_17.0 | all-reduce | flops 1024 | bytes 8192 | tf_op jit(solution)/shard_map/psum | solution.py:50
  263.0 12.3 %multiply_convert_fusion = bf16[512,8192]{1,0:T(8,128)(2,1)S(1)} fusion(f32[512,8192]{1,0:T(8,128)} %get-tuple-element.5, f32[512,8192]{1,0:T(8,128)} %get-tuple-element.7, f32[512]{0:T(512)S(1)} %divide_multiply_fusion, f32[8192]{0:T(1024)S(1)} %multiply_divide_fusion, f32[512]{0:T(512)S(1)} %get-tuple-element.3), kind=kLoop, calls=%fused_computation | loop fusion | flops 29360128 | bytes 41979904 | tf_op jit(solution)/shard_map/convert_element_type | solution.py:55
  275.3 3.2 copy-done.1
  278.5 5.5 %fusion.13 = f32[512,384]{1,0:T(8,128)} fusion(bf16[512,8192]{1,0:T(8,128)(2,1)S(1)} %multiply_convert_fusion, bf16[8192,384]{1,0:T(8,128)(2,1)S(1)} %bitcast.3, f32[8192]{0:T(1024)S(1)} %add_rsqrt_fusion.1), kind=kOutput, calls=%fused_computation.24 | convolution fusion | flops 3230662656 | bytes 15499264 | tf_op jit(solution)/shard_map/dot_general | solution.py:63
  284.0 0.0 all-reduce.6.cloned.1.call-update
  284.0 0.3 all-reduce.4.cloned.1.call-start
  284.3 12.7 %fusion.29 = f32[8192,384]{1,0:T(8,128)} fusion(bf16[512,8192]{1,0:T(8,128)(2,1)} %copy-done.1, bf16[512,384]{1,0:T(8,128)(2,1)S(1)} %copy-done.2, f32[512]{0:T(512)S(1)} %add_rsqrt_fusion.3), kind=kOutput, calls=%fused_computation.41 | convolution fusion | flops 3221815296 | bytes 21366784 | tf_op jit(solution)/shard_map/dot_general | solution.py:58
  297.1 0.0 all-reduce.4.cloned.1.call-update
  297.1 66.7 %all-reduce.6.cloned.1.call-done = f32[512,384]{1,0:T(8,128)} async-done(((f32[512,384]{1,0:T(8,128)}), f32[512,384]{1,0:T(8,128)}) %all-reduce.6.cloned.1.call-update) | async-done | bytes 786448 | tf_op jit(solution)/shard_map/psum | solution.py:64
  363.7 1.4 fusion.20
  365.1 2.1 fusion.23
  367.2 141.8 %all-reduce.4.cloned.1.call-done = f32[8192,384]{1,0:T(8,128)} async-done(((f32[8192,384]{1,0:T(8,128)}), f32[8192,384]{1,0:T(8,128)}) %all-reduce.4.cloned.1.call-update) | async-done | bytes 12582928 | tf_op jit(solution)/shard_map/psum | solution.py:61
  509.0 8.2 %fusion.4 = f32[8192]{0:T(1024)S(1)} fusion(f32[8192,384]{1,0:T(8,128)} %all-reduce.4.cloned.1.call-done, bf16[8192,384]{1,0:T(8,128)(2,1)} %param.6, f32[8192]{0:T(1024)S(1)} %add_rsqrt_fusion.1), kind=kLoop, calls=%fused_computation.16 | loop fusion | flops 12574720 | bytes 18939904 | tf_op jit(solution)/shard_map/reduce_sum | solution.py:27
  517.2 1.8 copy-done
  519.0 7.3 %fusion.7 = bf16[8192,384]{1,0:T(8,128)(2,1)} fusion(f32[8192,384]{1,0:T(8,128)S(1)} %copy-done, bf16[8192,384]{1,0:T(8,128)(2,1)} %param.6, f32[8192]{0:T(1024)S(1)} %fusion.4, f32[8192]{0:T(1024)S(1)} %add_rsqrt_fusion.1), kind=kLoop, calls=%fused_computation.19 | loop fusion | flops 18874368 | bytes 25231360 | tf_op jit(solution)/shard_map/convert_element_type | solution.py:62
  (26 shorter events, 0.1 us)
Async XLA Ops:
  7.2 11.0 %copy-start.3 = (bf16[512,384]{1,0:T(8,128)(2,1)S(1)}, bf16[512,384]{1,0:T(8,128)(2,1)}, u32[]{:S(2)}) copy-start(bf16[512,384]{1,0:T(8,128)(2,1)} %param.5) | copy-start | bytes 1179652
  7.2 11.0 %slice-start.2 = ((s8[6291456]{0:T(1024)(128)(4,1)}), s8[2097152]{0:T(1024)(128)(4,1)S(1)}, s32[]{:S(2)}) async-start(s8[6291456]{0:T(1024)(128)(4,1)} %bitcast.4), calls=%async_computation.4 | async-start | bytes 4194304
  7.2 356.6 %all-reduce.6.cloned.1.call-start = ((), (), s32[]{:S(2)}) async-start(), calls=%async_computation.1 | async-start | bytes 1572864 | tf_op jit(solution)/shard_map/psum | solution.py:64
  9.7 8.4 %slice-start.3 = ((s8[6291456]{0:T(1024)(128)(4,1)}), s8[4194304]{0:T(1024)(128)(4,1)S(1)}, s32[]{:S(2)}) async-start(s8[6291456]{0:T(1024)(128)(4,1)} %bitcast.4), calls=%async_computation.5 | async-start | bytes 8388608
  184.3 30.8 %copy-start.2 = (bf16[512,384]{1,0:T(8,128)(2,1)S(1)}, bf16[512,384]{1,0:T(8,128)(2,1)}, u32[]{:S(2)}) copy-start(bf16[512,384]{1,0:T(8,128)(2,1)} %param.4) | copy-start | bytes 1179652
  215.1 63.4 %slice-start = ((s8[6291456]{0:T(1024)(128)(4,1)}), s8[2097152]{0:T(1024)(128)(4,1)S(1)}, s32[]{:S(2)}) async-start(s8[6291456]{0:T(1024)(128)(4,1)} %bitcast.2), calls=%async_computation.2 | async-start | bytes 4194304
  263.0 15.5 %slice-start.1 = ((s8[6291456]{0:T(1024)(128)(4,1)}), s8[4194304]{0:T(1024)(128)(4,1)S(1)}, s32[]{:S(2)}) async-start(s8[6291456]{0:T(1024)(128)(4,1)} %bitcast.2), calls=%async_computation.3 | async-start | bytes 8388608
  275.3 3.2 copy-start.1
  284.0 225.0 %all-reduce.4.cloned.1.call-start = ((), (), s32[]{:S(2)}) async-start(), calls=%async_computation | async-start | bytes 25165824 | tf_op jit(solution)/shard_map/psum | solution.py:61
  509.0 10.0 %copy-start = (f32[8192,384]{1,0:T(8,128)S(1)}, f32[8192,384]{1,0:T(8,128)}, u32[]{:S(2)}) copy-start(f32[8192,384]{1,0:T(8,128)} %all-reduce.4.cloned.1.call-done) | copy-start | bytes 37748740
Sparse Core Ops, SparseCore 0:
  284.2 79.5 all-reduce.5
  366.2 142.7 all-reduce.3
where the time goes:
time: 534 us; the launch traced here: 533 us
  waiting for transfers between devices  208 us (39%)
  blocking collectives  188 us (35%)
  other arithmetic  80.3 us (15%)
  matrix products  36.8 us (7%)
  between operations  14.2 us (3%)
    psum x1, waiting for transfers between devices, on_device(): proto_back = lax.psum(proto_back, 'batch')  142 us
    psum x3, blocking collectives, on_device(): row_weight = 1.0 / (tok_all * lax.psum(row_part, 'proto'))  115 us
    psum x3, blocking collectives, on_device(): col_weight = 1.0 / (proto_all * lax.psum(col_part, 'batch'))  73 us
    psum x1, waiting for transfers between devices, on_device(): feat_back = lax.psum(feat_back, 'proto')  66.7 us
    reduce_sum x3, other arithmetic, on_device(): row_part = jnp.sum(teach_exp * col_weight[None, :], axis=1)  21.5 us
    dot_general x2, matrix products, similar(): lax.dot_general(left, right, (((1,), (1,)), ((), ())), preferred_element_...  18.5 us
    reduce_sum x2, other arithmetic, on_device(): col_part = jnp.sum(teach_exp * row_weight[:, None], axis=0)  16.6 us
    dot_general x1, matrix products, on_device(): lax.dot_general(delta, stud_unit, (((0,), (0,)), ((), ())), preferred_ele...  12.7 us
  transfers between devices with their start and end apart: 2, of which 2 were waited for; matrix products, arithmetic and copies ran while one was open for 3% of the time, Pallas kernels for 0%

commit v1 on v0

v1 whole, which is shorter than its diff:
```python
import jax
import jax.numpy as jnp
from jax import lax
from jax.sharding import PartitionSpec as P

ITERS = 3


eps = 1e-06
teacher_temp = 0.04
student_temp = 0.1


def unit_rows(matrix):
    values = matrix.astype(jnp.float32)
    scale = lax.rsqrt(jnp.sum(values * values, axis=1, keepdims=True) + eps)
    return (values * scale, scale)


def similar(left, right):
    return lax.dot_general(
        left, right, (((1,), (1,)), ((), ())), preferred_element_type=jnp.float32
    )


def back_norm(grad, unit, scale):
    return scale * (grad - unit * jnp.sum(grad * unit, axis=1, keepdims=True))


def on_device(student_feats, teacher_feats, student_protos, teacher_protos):
    parts = lax.axis_size("batch")
    tok_all = student_feats.shape[0] * parts
    proto_all = student_protos.shape[0] * lax.axis_size("proto")
    mine = student_protos.shape[0] // parts
    start = lax.axis_index("batch") * mine
    student_protos = lax.dynamic_slice_in_dim(student_protos, start, mine)
    teacher_protos = lax.dynamic_slice_in_dim(teacher_protos, start, mine)
    stud_float, stud_scale = unit_rows(student_feats)
    teach_float, _ = unit_rows(teacher_feats)
    proto_float, proto_scale = unit_rows(student_protos)
    anchor_float, _ = unit_rows(teacher_protos)
    teach_unit = lax.all_gather(teach_float.astype(jnp.bfloat16), "batch", tiled=True)
    stud_unit = lax.all_gather(stud_float.astype(jnp.bfloat16), "batch", tiled=True)
    proto_unit = proto_float.astype(jnp.bfloat16)
    anchor_unit = anchor_float.astype(jnp.bfloat16)
    teach_exp = jnp.exp(similar(anchor_unit, teach_unit) / teacher_temp)
    exp_logits = jnp.exp(similar(proto_unit, stud_unit) / student_temp)
    row_weight = jnp.ones((tok_all,), jnp.float32)
    for sweep in range(ITERS):
        col_sum = jnp.sum(teach_exp * row_weight[None, :], axis=1)
        col_weight = 1.0 / (proto_all * col_sum)
        row_part = jnp.sum(teach_exp * col_weight[:, None], axis=0)
        if sweep == ITERS - 1:
            row_part = jnp.stack([row_part, jnp.sum(exp_logits, axis=0)])
            row_part, total = lax.psum(row_part, ("batch", "proto"))
        else:
            row_part = lax.psum(row_part, ("batch", "proto"))
        row_weight = 1.0 / (tok_all * row_part)
    targets = tok_all * teach_exp * row_weight[None, :] * col_weight[:, None]
    delta = ((exp_logits / total[None, :] - targets) / (student_temp * tok_all)).astype(
        jnp.bfloat16
    )
    proto_back = jnp.dot(delta, stud_unit, preferred_element_type=jnp.float32)
    grad_proto = back_norm(proto_back, proto_float, proto_scale).astype(jnp.bfloat16)
    grad_proto = lax.all_gather(grad_proto, "batch", tiled=True)
    feat_back = lax.dot_general(
        delta, proto_unit, (((0,), (0,)), ((), ())), preferred_element_type=jnp.float32
    )
    feat_back = lax.psum_scatter(feat_back, "batch", tiled=True)
    feat_back = lax.psum(feat_back, "proto")
    grad_student = back_norm(feat_back, stud_float, stud_scale).astype(jnp.bfloat16)
    return (grad_proto, grad_student)


def solution(mesh):
    in_specs = (P("batch", None), P("batch", None), P("proto", None), P("proto", None))
    out_specs = (P("proto", None), P("batch", None))
    return jax.shard_map(
        on_device, mesh=mesh, in_specs=in_specs, out_specs=out_specs, check_vma=False
    )
```

time: 534 us -> 496 us (0.929)
  waiting for transfers between devices: 208 us -> 178 us
  other arithmetic: 80.3 us -> 60.2 us
  local copies, waits for them, and re-layouts: 5.06 us -> 13.3 us
    psum x1 -> x0, waiting for transfers between devices: 142 us -> none  [on_device(): proto_back = lax.psum(proto_back, 'batch')]
    all_gather x0 -> x3, waiting for transfers between devices: none -> 66.3 us  [the longest x1 42.2 us: on_device(): grad_proto = lax.all_gather(grad_proto, 'batch', tiled=True)]
    reduce_scatter x0 -> x1, waiting for transfers between devices: none -> 31.2 us  [on_device(): feat_back = lax.psum_scatter(feat_back, 'batch', tiled=True)]
    psum x1, waiting for transfers between devices: 66.7 us -> 80.8 us  [on_device(): feat_back = lax.psum(feat_back, 'proto')]
    reduce_sum x2 -> x1, other arithmetic: 9.56 us -> 1.38 us  [back_norm(): return scale * (grad - unit * jnp.sum(grad * unit, axis=1, keepdims=True))]
    unnamed x16 -> x6, local copies, waits for them, and re-layouts: 5.06 us -> 12.1 us
    reduce_sum x4, other arithmetic: 10.8 us -> 3.84 us  [unit_rows(): scale = lax.rsqrt(jnp.sum(values * values, axis=1, keepdims=True) + eps)]
    convert_element_type x1, other arithmetic: 7.27 us -> 1.2 us  [on_device(): back_norm(proto_back, proto_float, proto_scale).astype(jnp.bfloat16)]
  transfers between devices with their start and end apart: 2 -> 5, of which waited for: 2 -> 4; matrix products, arithmetic and copies ran while one was open for 3% -> 14% of each run, Pallas kernels for 0% -> 0%
where the time goes in v1:
time: 496 us; the launch traced here: 495 us
  blocking collectives  192 us (39%)
  waiting for transfers between devices  178 us (36%)
  other arithmetic  60.2 us (12%)
  matrix products  36.8 us (7%)
  between operations  13.9 us (3%)
  local copies, waits for them, and re-layouts  13.3 us (3%)
    psum x2, blocking collectives, on_device(): row_part = lax.psum(row_part, ('batch', 'proto'))  130 us
    psum x1, waiting for transfers between devices, on_device(): feat_back = lax.psum(feat_back, 'proto')  80.8 us
    psum x1, blocking collectives, on_device(): row_part, total = lax.psum(row_part, ('batch', 'proto'))  62.4 us
    all_gather x1, waiting for transfers between devices, on_device(): grad_proto = lax.all_gather(grad_proto, 'batch', tiled=True)  42.2 us
    reduce_scatter x1, waiting for transfers between devices, on_device(): feat_back = lax.psum_scatter(feat_back, 'batch', tiled=True)  31.2 us
    all_gather x1, waiting for transfers between devices, on_device(): lax.all_gather(teach_float.astype(jnp.bfloat16), 'batch', tiled=True)  24.1 us
    dot_general x2, matrix products, similar(): lax.dot_general(left, right, (((1,), (1,)), ((), ())), preferred_element_...  23.2 us
    reduce_sum x3, other arithmetic, on_device(): row_part = jnp.sum(teach_exp * col_weight[:, None], axis=0)  21.5 us
  transfers between devices with their start and end apart: 5, of which 4 were waited for; matrix products, arithmetic and copies ran while one was open for 14% of the time, Pallas kernels for 0%

profile of v1, /device:TPU:0, one launch (start us, length us, event | category | flops | bytes accessed | tf_op | source)
XLA Modules:
  0.0 495.3 jit_solution(9439437452248005092)
XLA Ops:
  7.2 1.1 fusion.19
  8.4 1.9 fusion.20
  10.3 0.0 all-gather.4.cloned.1.call-start
  10.3 1.1 fusion.18
  11.5 1.9 fusion.13
  13.4 1.4 fusion.9
  14.8 1.2 constant_dynamic-slice_fusion
  16.0 0.3 copy.8
  16.3 0.2 fusion.8
  16.5 24.1 %all-gather.6.cloned.1.call-done = bf16[4096,384]{1,0:T(8,128)(2,1)} async-done(((bf16[512,384]{1,0:T(8,128)(2,1)}), bf16[4096,384]{1,0:T(8,128)(2,1)}) %all-gather.6.cloned.1.call-update) | async-done | bytes 3145744 | tf_op jit(solution)/shard_map/all_gather | solution.py:42
  40.6 13.0 %fusion.32 = (f32[1024]{0:T(1024)S(1)}, f32[1024,4096]{1,0:T(8,128)}) fusion(bf16[4096,384]{1,0:T(8,128)(2,1)} %all-gather.6.cloned.1.call-done, f32[1024]{0:T(1024)S(1)} %add_rsqrt_fusion, bf16[8192,384]{1,0:T(8,128)(2,1)} %param.7, s32[]{:T(128)S(6)} %select_n.4), kind=kOutput, calls=%fused_computation.57 | convolution fusion | flops 3230792704 | bytes 20717572 | tf_op jit(solution)/shard_map/dot_general | solution.py:21
  53.6 7.2 %multiply_reduce_fusion.4 = f32[4096]{0:T(1024)S(1)} fusion(f32[1024,4096]{1,0:T(8,128)} %get-tuple-element.9, f32[1024]{0:T(1024)S(1)} %multiply_divide_fusion.4), kind=kLoop, calls=%fused_computation.5 | loop fusion | flops 8384512 | bytes 16797696 | tf_op jit(solution)/shard_map/reduce_sum | solution.py:52
  60.8 66.0 %psum.28 = f32[4096]{0:T(1024)S(1)} all-reduce(f32[4096]{0:T(1024)S(1)} %multiply_reduce_fusion.4), channel_id=1, replica_groups=mesh['batch'=8,'proto'=16] {'batch','proto'}, use_global_device_ids=true, to_apply=%region_6.0 | all-reduce | flops 4096 | bytes 32768 | tf_op jit(solution)/shard_map/psum | solution.py:57
  126.8 7.1 %multiply_reduce_fusion.3 = f32[1024]{0:T(1024)S(1)} fusion(f32[1024,4096]{1,0:T(8,128)} %get-tuple-element.9, f32[4096]{0:T(1024)S(1)} %multiply_divide_fusion.1), kind=kLoop, calls=%fused_computation.4 | loop fusion | flops 8387584 | bytes 16797696 | tf_op jit(solution)/shard_map/reduce_sum | solution.py:50
  133.8 7.2 %multiply_reduce_fusion.2 = f32[4096]{0:T(1024)S(1)} fusion(f32[1024,4096]{1,0:T(8,128)} %get-tuple-element.9, f32[1024]{0:T(1024)S(1)} %multiply_divide_fusion.3), kind=kLoop, calls=%fused_computation.3 | loop fusion | flops 8384512 | bytes 16797696 | tf_op jit(solution)/shard_map/reduce_sum | solution.py:52
  141.0 64.0 %psum.29 = f32[4096]{0:T(1024)S(1)} all-reduce(f32[4096]{0:T(1024)S(1)} %multiply_reduce_fusion.2), channel_id=1, replica_groups=mesh['batch'=8,'proto'=16] {'batch','proto'}, use_global_device_ids=true, to_apply=%region_9.0 | all-reduce | flops 4096 | bytes 32768 | tf_op jit(solution)/shard_map/psum | solution.py:57
  205.0 7.1 %multiply_reduce_fusion.1 = f32[1024]{0:T(1024)S(1)} fusion(f32[1024,4096]{1,0:T(8,128)} %get-tuple-element.9, f32[4096]{0:T(1024)S(1)} %multiply_divide_fusion), kind=kLoop, calls=%fused_computation.2 | loop fusion | flops 8387584 | bytes 16797696 | tf_op jit(solution)/shard_map/reduce_sum | solution.py:50
  212.1 7.2 %multiply_reduce_fusion = f32[4096]{0:T(1024)S(1)} fusion(f32[1024,4096]{1,0:T(8,128)} %get-tuple-element.9, f32[1024]{0:T(1024)S(1)} %multiply_divide_fusion.2), kind=kLoop, calls=%fused_computation.1 | loop fusion | flops 8384512 | bytes 16797696 | tf_op jit(solution)/shard_map/reduce_sum | solution.py:52
  219.3 10.3 %fusion = (f32[4096]{0:T(1024)S(1)}, f32[1024,4096]{1,0:T(8,128)}) fusion(bf16[4096,384]{1,0:T(8,128)(2,1)} %all-gather.4.cloned.1.call-done, bf16[1024,384]{0,1:T(8,128)(2,1)S(1)} %copy.8, f32[1024]{0:T(1024)S(1)} %add_rsqrt_fusion.1), kind=kOutput, calls=%fused_computation.8 | convolution fusion | flops 3230789632 | bytes 20729856 | tf_op jit(solution)/shard_map/dot_general | solution.py:21
  229.6 62.4 %psum.30 = f32[2,4096]{1,0:T(2,128)S(1)} all-reduce(f32[2,4096]{1,0:T(2,128)S(1)} %pad_maximum_fusion), channel_id=1, replica_groups=mesh['batch'=8,'proto'=16] {'batch','proto'}, use_global_device_ids=true, to_apply=%region_13.0 | all-reduce | flops 8192 | bytes 65536 | tf_op jit(solution)/shard_map/psum | solution.py:55
  292.1 12.1 %multiply_convert_fusion = bf16[1024,4096]{1,0:T(8,128)(2,1)S(1)} fusion(f32[1024,4096]{1,0:T(8,128)} %get-tuple-element.9, f32[1024,4096]{1,0:T(8,128)} %get-tuple-element.7, f32[4096]{0:T(1024)S(1)} %bitcast.10, f32[4096]{0:T(1024)S(1)} %bitcast.9, f32[1024]{0:T(1024)S(1)} %multiply_divide_fusion.2), kind=kLoop, calls=%fused_computation | loop fusion | flops 29360128 | bytes 41979904 | tf_op jit(solution)/shard_map/convert_element_type | solution.py:60
  304.2 3.2 copy-done
  307.4 6.6 %fusion.24 = f32[4096,384]{1,0:T(8,128)} fusion(bf16[1024,4096]{1,0:T(8,128)(2,1)S(1)} %multiply_convert_fusion, bf16[1024,384]{0,1:T(8,128)(2,1)S(1)} %copy.8, f32[1024]{0:T(1024)S(1)} %add_rsqrt_fusion.1), kind=kOutput, calls=%fused_computation.39 | convolution fusion | flops 3222405120 | bytes 15470592 | tf_op jit(solution)/shard_map/dot_general | solution.py:66
  314.0 0.3 all-gather.8.cloned.1.call-start
  314.3 6.9 %fusion.4 = (f32[1024]{0:T(1024)S(1)}, f32[1024,384]{0,1:T(8,128)S(1)}) fusion(bf16[1024,384]{0,1:T(8,128)(2,1)S(1)} %copy.8, f32[1024]{0:T(1024)S(1)} %add_rsqrt_fusion.1, bf16[1024,4096]{1,0:T(8,128)(2,1)} %copy-done, bf16[4096,384]{1,0:T(8,128)(2,1)} %all-gather.4.cloned.1.call-done), kind=kOutput, calls=%fused_computation.16 | convolution fusion | flops 3222797312 | bytes 13901824 | tf_op jit(solution)/shard_map/dot_general | solution.py:63
  321.2 1.2 fusion.7
  322.5 31.2 %reduce-scatter.2.cloned.1.call-done = f32[512,384]{1,0:T(8,128)} async-done(((f32[4096,384]{1,0:T(8,128)}), f32[512,384]{1,0:T(8,128)}) %reduce-scatter.2.cloned.1.call-update) | async-done | bytes 786448 | tf_op jit(solution)/shard_map/reduce_scatter | solution.py:69
  353.7 42.2 %all-gather.8.cloned.1.call-done = bf16[8192,384]{0,1:T(8,128)(2,1)} async-done(((bf16[1024,384]{0,1:T(8,128)(2,1)}), bf16[8192,384]{0,1:T(8,128)(2,1)}) %all-gather.8.cloned.1.call-update) | async-done | bytes 6291472 | tf_op jit(solution)/shard_map/all_gather | solution.py:65
  395.9 8.6 %copy.7 = bf16[8192,384]{1,0:T(8,128)(2,1)} copy(bf16[8192,384]{0,1:T(8,128)(2,1)} %all-gather.8.cloned.1.call-done) | data formatting | bytes 12582912
  404.5 80.8 %all-reduce.2.cloned.1.call-done = f32[512,384]{1,0:T(8,128)} async-done(((f32[512,384]{1,0:T(8,128)}), f32[512,384]{1,0:T(8,128)}) %all-reduce.2.cloned.1.call-update) | async-done | bytes 786448 | tf_op jit(solution)/shard_map/psum | solution.py:70
  485.3 1.4 fusion.14
  486.7 2.1 fusion.17
  (23 shorter events, 0.4 us)
Async XLA Ops:
  7.2 33.5 %all-gather.6.cloned.1.call-start = ((), (), s32[]{:S(2)}) async-start(), calls=%async_computation.2 | async-start | bytes 3538944 | tf_op jit(solution)/shard_map/all_gather | solution.py:42
  10.3 209.0 %all-gather.4.cloned.1.call-start = ((), (), s32[]{:S(2)}) async-start(), calls=%async_computation.1 | async-start | bytes 3538944 | tf_op jit(solution)/shard_map/all_gather | solution.py:43
  13.4 340.3 %reduce-scatter.2.cloned.1.call-start = ((), (), s32[]{:S(2)}) async-start(), calls=%async_computation.4 | async-start | bytes 7077888 | tf_op jit(solution)/shard_map/reduce_scatter | solution.py:69
  304.2 3.2 copy-start
  314.0 81.8 %all-gather.8.cloned.1.call-start = ((), (), s32[]{:S(2)}) async-start(), calls=%async_computation.3 | async-start | bytes 7077888 | tf_op jit(solution)/shard_map/all_gather | solution.py:65
  322.5 162.9 %all-reduce.2.cloned.1.call-start = ((), (), s32[]{:S(2)}) async-start(), calls=%async_computation.5 | async-start | bytes 1572864 | tf_op jit(solution)/shard_map/psum | solution.py:70
  353.7 131.6 %copy-start.1 = (bf16[512,384]{1,0:T(8,128)(2,1)S(1)}, bf16[512,384]{1,0:T(8,128)(2,1)}, u32[]{:S(2)}) copy-start(bf16[512,384]{1,0:T(8,128)(2,1)} %param.4) | copy-start | bytes 1179652
Sparse Core Ops, SparseCore 0:
  10.4 30.1 all-gather.5
  42.9 27.7 all-gather.3
  314.2 39.4 reduce-scatter.1
  355.2 40.6 all-gather.7
  399.0 86.3 all-reduce.1

commit v2 on v0

v2 whole, which is shorter than its diff:
```python
import functools

import jax
import jax.numpy as jnp
from jax import lax
from jax.experimental import pallas as pl
from jax.experimental.pallas import tpu as pltpu
from jax.sharding import PartitionSpec as P

ITERS = 3
eps = 1e-06
teacher_temp = 0.04
student_temp = 0.1
LOG2E = 1.4426950408889634
F32 = jnp.float32
BF = jnp.bfloat16
MESH = pl.DeviceIdType.MESH
CH = 128


def nt(left, right):
    return lax.dot_general(
        left, right, (((1,), (1,)), ((), ())), preferred_element_type=F32
    )


def nn(left, right):
    return jnp.dot(left, right, preferred_element_type=F32)


def tn(left, right):
    return lax.dot_general(
        left, right, (((0,), (0,)), ((), ())), preferred_element_type=F32
    )


def loop(count, body):
    def step(i, carry):
        body(i)
        return carry

    lax.fori_loop(0, count, step, 0)


def rows(start, size):
    return pl.ds(pl.multiple_of(start, size), size)


def unit_rows(values):
    values = values.astype(F32)
    scale = lax.rsqrt(jnp.sum(values * values, axis=1, keepdims=True) + eps)
    return values * scale, scale


def back_norm(grad, unit, scale):
    return scale * (grad - unit * jnp.sum(grad * unit, axis=1, keepdims=True))


def kernel(
    nb, nq,
    sf, tf, sp_hbm, tp_hbm,
    gp_out, gs_out,
    t_all, s_all, sp, anchor, pu, e, s, cs, tot, fa, fb, fbb, st, sr, gpb, ccol,
    r16, c16, w_src, w_mid, w_g1, w_g2, w_out, cx, yzr, sumf, xs, xr, gsb,
    lsem, t_s, t_r, tf_s, tf_r, s_s, s_r, sf_s, sf_r,
    a1_s, a1_r, a2_s, a2_r, g_s, g_r, f_s, f_r, sib_s, sib_r, own_s,
    cx_s, cx_r, yz_s, yz_r, xr_s, xr_r, gs_s, gs_r,
):
    nx = nb // 2
    tl, depth = sf.shape
    tokens = tl * nb
    pl_rows = sp.shape[0]
    protos = pl_rows * nb * nq
    chunks = pl_rows // CH
    wide = tokens // 128
    piece = tl // nq
    plane = 2 * tl
    b, p = lax.axis_index("batch"), lax.axis_index("proto")
    x, c = b // 2, lax.rem(b, 2)

    def bat(dx, dc):
        return lax.rem(x + dx, nx) * 2 + lax.rem(c + dc, 2)

    def remote(src, dst, ss, rs, to):
        return pltpu.make_async_remote_copy(
            src, dst, ss, rs, device_id=to, device_id_type=MESH
        )

    sibling = (bat(0, 1), p)

    barrier = pltpu.get_barrier_semaphore()
    for j in range(1, nb):
        pl.semaphore_signal(
            barrier, inc=1, device_id=(lax.rem(b + j, nb), p), device_id_type=MESH
        )
    for j in range(1, nq):
        pl.semaphore_signal(
            barrier, inc=1, device_id=(b, lax.rem(p + j, nq)), device_id_type=MESH
        )
    load_t = pltpu.make_async_copy(tp_hbm.at[rows(b * pl_rows, pl_rows)], anchor, lsem.at[0])
    load_s = pltpu.make_async_copy(sp_hbm.at[rows(b * pl_rows, pl_rows)], sp, lsem.at[1])
    load_t.start()
    load_s.start()

    def norm_into(src, dst, start, count):
        def body(i):
            unit, _ = unit_rows(src[rows(i * 128, 128), :])
            dst[rows(start + i * 128, 128), :] = unit.astype(BF)

        loop(count // 128, body)

    norm_into(tf, t_all, b * tl, tl)
    pl.semaphore_wait(barrier, nb + nq - 2)

    def sends(buf, ss, rs):
        mine = buf.at[rows(b * tl, tl)]
        out = [remote(mine, mine, ss.at[0], rs.at[0], sibling)]
        for dx in range(1, nx):
            out.append(remote(mine, mine, ss.at[dx], rs.at[dx], (bat(dx, 0), p)))
        return out

    def forward(buf, ss, rs, dx):
        block = buf.at[rows(bat(nx - dx, 0) * tl, tl)]
        return remote(block, block, ss.at[dx], rs.at[dx], sibling)

    order = [0, 1, nx - 1] + list(range(2, nx - 1))
    order = order[:1] + [d for i, d in enumerate(order[1:]) if d not in order[1:][:i]]
    t_sends = sends(t_all, t_s, t_r)
    for dx in order:
        t_sends[dx].start()
    norm_into(sf, s_all, b * tl, tl)
    load_t.wait()
    norm_into(anchor, anchor, 0, pl_rows)
    load_s.wait()
    norm_into(sp, pu, 0, pl_rows)

    def exp_plane(left, right, out, dx, factor, accumulate):
        off = lax.rem(x + nx - dx, nx) * plane
        cols = rows(off, plane)

        def body(i):
            sl = rows(i * 256, 256)
            value = jnp.exp2(nt(left[sl, :], right[cols, :]) * factor)
            out[sl, cols] = value.astype(BF)
            accumulate(value, sl, cols, dx)

        loop(pl_rows // 256, body)

    def col_acc(value, sl, cols, dx):
        acc = value[:, 0:128]
        for q in range(1, plane // 128):
            acc = acc + value[:, q * 128 : (q + 1) * 128]
        if dx == 0:
            cs[sl, :] = acc
        else:
            cs[sl, :] += acc

    def row_acc(value, sl, cols, dx):
        tot[:, cols] += jnp.sum(value.reshape(32, 8, plane), axis=0)

    def arrive(buf, ds, ss, rs, fs, fr, dx):
        if dx == 0:
            ds[0].wait_recv()
        else:
            ds[dx].wait_recv()
            forward(buf, fs, fr, dx).start()

    def arrived(buf, fs, fr, dx):
        if dx:
            forward(buf, fs, fr, dx).wait_recv()

    for dx in order:
        arrive(t_all, t_sends, t_s, t_r, tf_s, tf_r, dx)
        arrived(t_all, tf_s, tf_r, dx)
        exp_plane(anchor, t_all, e, dx, LOG2E / teacher_temp, col_acc)
    s_sends = sends(s_all, s_s, s_r)
    for dx in order:
        s_sends[dx].start()

    half = lax.broadcasted_iota(jnp.int32, (16, 128), 0) < 8

    def split_into(dst, j, row):
        high = row.astype(BF).astype(F32)
        dst[:, j * 128 : (j + 1) * 128] = jnp.where(half, high, row - high).astype(BF)

    def reduce_start(n, height):
        h = slice(0, height)
        ds = [
            remote(w_src.at[n, h], w_g1.at[n, j - 1, h], a1_s.at[n, j - 1],
                   a1_r.at[n, j - 1], (lax.rem(b + j, nb), p))
            for j in range(1, nb)
        ]
        for d in ds:
            d.start()
        return ds

    def reduce_middle(n, height, ds):
        h = slice(0, height)
        for d in ds:
            d.wait_recv()
        value = w_src[n, h]
        for j in range(nb - 1):
            value = value + w_g1[n, j, h]
        w_mid[n, h] = value
        out = [
            remote(w_mid.at[n, h], w_g2.at[n, j - 1, h], a2_s.at[n, j - 1],
                   a2_r.at[n, j - 1], (b, lax.rem(p + j, nq)))
            for j in range(1, nq)
        ]
        for d in out:
            d.start()
        return out

    def reduce_end(n, height, ds):
        h = slice(0, height)
        for d in ds:
            d.wait_recv()
        value = w_mid[n, h]
        for j in range(nq - 1):
            value = value + w_g2[n, j, h]
        return value

    def col_weights(j, sums):
        return 1.0 / (protos * sums)

    def row_pass(n):
        out = nn(c16[...], e[...])
        line = out[0:1, :] + out[8:9, :]
        for j in range(wide):
            w_src[n, j : j + 1, :] = line[:, j * 128 : (j + 1) * 128]

    def col_pass(weights):
        for j in range(wide):
            split_into(r16, j, weights[j : j + 1, :])
        out = nt(r16[...], e[...])
        line = 1.0 / (protos * (out[0:1, :] + out[8:9, :]))
        return [line[:, j * 128 : (j + 1) * 128] for j in range(pl_rows // 128)]

    tot[...] = jnp.zeros_like(tot)

    def student_plane(dx):
        arrived(s_all, sf_s, sf_r, dx)
        exp_plane(pu, s_all, s, dx, LOG2E / student_temp, row_acc)

    pending = []
    for j in range(pl_rows // 128):
        sums = jnp.sum(cs[j * 128 : (j + 1) * 128, :].T, axis=0, keepdims=True)
        split_into(c16, j, 1.0 / (protos * sums))
    row_pass(0)
    ds = reduce_start(0, wide)
    pending += ds
    arrive(s_all, s_sends, s_s, s_r, sf_s, sf_r, 0)
    student_plane(0)
    ds = reduce_middle(0, wide, ds)
    pending += ds
    weights = 1.0 / (tokens * reduce_end(0, wide, ds))
    for dx in order[1:]:
        arrive(s_all, s_sends, s_s, s_r, sf_s, sf_r, dx)
    for j, line in enumerate(col_pass(weights)):
        split_into(c16, j, line)
    row_pass(1)
    ds = reduce_start(1, wide)
    pending += ds
    for dx in order[1:3]:
        student_plane(dx)
    ds = reduce_middle(1, wide, ds)
    pending += ds
    for dx in order[3:]:
        student_plane(dx)
    weights = 1.0 / (tokens * reduce_end(1, wide, ds))
    lines = col_pass(weights)
    for j, line in enumerate(lines):
        split_into(c16, j, line)
    row_pass(2)
    line = jnp.sum(tot[...], axis=0, keepdims=True)
    for j in range(wide):
        w_src[2, wide + j : wide + j + 1, :] = line[:, j * 128 : (j + 1) * 128]
    ds = reduce_start(2, 2 * wide)
    pending += ds
    for j, line in enumerate(lines):
        ccol[j * 128 : (j + 1) * 128, :] = jnp.broadcast_to(line, (128, 128)).T

    def feat_part(left, right, out):
        def body(j):
            cols = rows(j * 512, 512)
            out[cols, :] = tn(left[:, cols], right[...])

        loop(tokens // 512, body)

    feat_part(s, pu, fa)
    ds = reduce_middle(2, 2 * wide, ds)
    pending += ds

    def scale_protos(j):
        sl = rows(j * 128, 128)
        anchor[sl, :] = (ccol[sl, 0:1] * pu[sl, :].astype(F32)).astype(BF)

    loop(pl_rows // 128, scale_protos)
    feat_part(e, anchor, fb)
    value = reduce_end(2, 2 * wide, ds)
    w_out[0:wide, :] = (1.0 / student_temp) / (tokens * value[0:wide])
    w_out[wide : 2 * wide, :] = 1.0 / (student_temp * tokens * value[wide : 2 * wide])

    def apply_weights(j):
        sl = rows(j * 128, 128)
        rcol = jnp.broadcast_to(w_out[pl.ds(j, 1), :], (128, 128)).T[:, 0:1]
        tcol = jnp.broadcast_to(w_out[pl.ds(wide + j, 1), :], (128, 128)).T[:, 0:1]
        stud = s_all[sl, :].astype(F32)
        sr[sl, :] = (stud * rcol).astype(BF)
        st[sl, :] = (stud * tcol).astype(BF)
        fbb[sl, :] = (fa[sl, :] * tcol - fb[sl, :] * rcol).astype(BF)

    loop(wide, apply_weights)

    cx_d = []
    for xx in range(nx):
        d = remote(
            fbb.at[rows((xx * 2 + 1 - c) * tl, tl)], cx.at[xx],
            cx_s.at[xx], cx_r.at[xx], sibling,
        )
        d.start()
        cx_d.append(d)

    def block_rows(block, q):
        return rows(block * pl_rows + q * CH, CH)

    def half_rows(block, q, k):
        return rows(block * pl_rows + q * CH + k * (CH // 2), CH // 2)

    def own_copy(q):
        return pltpu.make_async_copy(
            gpb.at[rows(q * CH, CH)], gp_out.at[block_rows(b, q)], own_s.at[q]
        )

    def chunk_send(q, k):
        to = (bat(1, 0), p) if k == 0 else (bat(nx - 1, 0), p)
        return remote(
            gpb.at[rows(q * CH, CH)], gp_out.at[block_rows(b, q)],
            g_s.at[k, q], g_r.at[k, q], to,
        )

    def chunk_forward(q, k):
        block = bat(nx - 1, 0) if k == 0 else bat(1, 0)
        to = (bat(1, 0), p) if k == 0 else (bat(nx - 1, 0), p)
        part = gp_out.at[half_rows(block, q, k)]
        return remote(part, part, f_s.at[k, q], f_r.at[k, q], to)

    def chunk_sibling(q, k):
        block = bat((0, nx - 1, 1, 2)[k], 0)
        part = gp_out.at[block_rows(block, q)]
        src = gpb.at[rows(q * CH, CH)] if k == 0 else part
        return remote(src, part, sib_s.at[k, q], sib_r.at[k, q], sibling)

    def chunk_compute(q):
        sl = rows(q * CH, CH)
        back = nn(s[sl, :], st[...]) - ccol[sl, 0:1] * nn(e[sl, :], sr[...])
        unit, scale = unit_rows(sp[sl, :])
        gpb[sl, :] = back_norm(back, unit, scale).astype(BF)
        chunk_send(q, 0).start()
        chunk_send(q, 1).start()
        chunk_sibling(q, 0).start()
        own_copy(q).start()

    def chunk_recv(q):
        for k in range(2):
            chunk_send(q, k).wait_recv()
            chunk_forward(q, k).start()
            chunk_sibling(q, 1 + k).start()

    def chunk_last(q):
        for k in range(2):
            chunk_forward(q, k).wait_recv()
        chunk_sibling(q, 3).start()

    loop(3, chunk_compute)

    for d in cx_d:
        d.wait_recv()
    for xx in range(nx):
        def add_sibling(i, xx=xx):
            sl = rows(i * 128, 128)
            mine = fbb[rows((xx * 2 + c) * tl + i * 128, 128), :].astype(F32)
            cx[xx, sl, :] = (mine + cx[xx, sl, :].astype(F32)).astype(BF)

        loop(tl // 128, add_sibling)
    yz_d = []
    for j in range(1, nq):
        d = remote(
            cx.at[:, rows(lax.rem(p + j, nq) * piece, piece), :], yzr.at[j - 1],
            yz_s.at[j - 1], yz_r.at[j - 1], (b, lax.rem(p + j, nq)),
        )
        d.start()
        yz_d.append(d)

    loop(chunks - 3, lambda i: chunk_compute(i + 3))
    loop(chunks, chunk_recv)
    for d in yz_d:
        d.wait_recv()
    value = cx[:, rows(p * piece, piece), :].astype(F32)
    for j in range(nq - 1):
        value = value + yzr[j].astype(F32)
    sumf[...] = value
    xs[...] = value.astype(BF)
    xr_d = []
    for dx in range(1, nx):
        d = remote(
            xs.at[lax.rem(x + dx, nx)], xr.at[dx - 1],
            xr_s.at[dx - 1], xr_r.at[dx - 1], (bat(dx, 0), p),
        )
        d.start()
        xr_d.append(d)
    loop(chunks, chunk_last)
    for d in xr_d:
        d.wait_recv()
    value = sumf[x]
    for dx in range(nx - 1):
        value = value + xr[dx].astype(F32)
    own = rows(p * piece, piece)
    unit, scale = unit_rows(sf[own, :])
    gsb[...] = back_norm(value, unit, scale).astype(BF)
    gs_out[own, :] = gsb[...]
    gs_d = []
    for j in range(1, nq):
        d = remote(
            gsb, gs_out.at[own], gs_s.at[j - 1], gs_r.at[j - 1], (b, lax.rem(p + j, nq))
        )
        d.start()
        gs_d.append(d)

    for d in t_sends + s_sends + pending + cx_d + yz_d + xr_d + gs_d:
        d.wait_send()
    for dx in range(1, nx):
        forward(t_all, tf_s, tf_r, dx).wait_send()
        forward(s_all, sf_s, sf_r, dx).wait_send()

    def drain(q):
        own_copy(q).wait()
        for k in range(2):
            chunk_send(q, k).wait_send()
            chunk_forward(q, k).wait_send()
        for k in range(4):
            chunk_sibling(q, k).wait()

    loop(chunks, drain)
    for d in gs_d:
        d.wait_recv()


def on_device(nb, nq, student_feats, teacher_feats, student_protos, teacher_protos):
    tl, depth = student_feats.shape
    pl_rows = student_protos.shape[0] // nb
    tokens = tl * nb
    chunks = pl_rows // CH
    wide = tokens // 128
    nx = nb // 2
    piece = tl // nq
    vm = pltpu.VMEM
    dma = pltpu.SemaphoreType.DMA
    scratch = [
        vm((tokens, depth), BF),
        vm((tokens, depth), BF),
        vm((pl_rows, depth), BF),
        vm((pl_rows, depth), BF),
        vm((pl_rows, depth), BF),
        vm((pl_rows, tokens), BF),
        vm((pl_rows, tokens), BF),
        vm((pl_rows, 128), F32),
        vm((8, tokens), F32),
        vm((tokens, depth), F32),
        vm((tokens, depth), F32),
        vm((tokens, depth), BF),
        vm((tokens, depth), BF),
        vm((tokens, depth), BF),
        vm((pl_rows, depth), BF),
        vm((pl_rows, 128), F32),
        vm((16, tokens), BF),
        vm((16, pl_rows), BF),
        vm((ITERS, 2 * wide, 128), F32),
        vm((ITERS, 2 * wide, 128), F32),
        vm((ITERS, nb - 1, 2 * wide, 128), F32),
        vm((ITERS, nq - 1, 2 * wide, 128), F32),
        vm((2 * wide, 128), F32),
        vm((nx, tl, depth), BF),
        vm((nq - 1, nx, piece, depth), BF),
        vm((nx, piece, depth), F32),
        vm((nx, piece, depth), BF),
        vm((nx - 1, piece, depth), BF),
        vm((piece, depth), BF),
        dma((2,)),
        dma((nx,)), dma((nx,)), dma((nx,)), dma((nx,)),
        dma((nx,)), dma((nx,)), dma((nx,)), dma((nx,)),
        dma((ITERS, nb - 1)), dma((ITERS, nb - 1)),
        dma((ITERS, nq - 1)), dma((ITERS, nq - 1)),
        dma((2, chunks)), dma((2, chunks)), dma((2, chunks)), dma((2, chunks)),
        dma((4, chunks)), dma((4, chunks)), dma((chunks,)),
        dma((nx,)), dma((nx,)),
        dma((nq - 1,)), dma((nq - 1,)),
        dma((nx - 1,)), dma((nx - 1,)),
        dma((nq - 1,)), dma((nq - 1,)),
    ]
    in_vmem = pl.BlockSpec(memory_space=pltpu.VMEM)
    anywhere = pl.BlockSpec(memory_space=pl.ANY)
    return pl.pallas_call(
        functools.partial(kernel, nb, nq),
        out_shape=[
            jax.ShapeDtypeStruct(student_protos.shape, BF),
            jax.ShapeDtypeStruct(student_feats.shape, BF),
        ],
        in_specs=[in_vmem, in_vmem, anywhere, anywhere],
        out_specs=[anywhere, in_vmem],
        scratch_shapes=scratch,
        compiler_params=pltpu.CompilerParams(
            collective_id=0, has_side_effects=True, vmem_limit_bytes=62 << 20
        ),
        name="prototype_head",
    )(student_feats, teacher_feats, student_protos, teacher_protos)


def solution(mesh):
    nb, nq = mesh.shape["batch"], mesh.shape["proto"]
    in_specs = (P("batch", None), P("batch", None), P("proto", None), P("proto", None))
    out_specs = (P("proto", None), P("batch", None))
    return jax.shard_map(
        functools.partial(on_device, nb, nq),
        mesh=mesh, in_specs=in_specs, out_specs=out_specs, check_vma=False,
    )
```

time: 534 us -> 149 us (0.28)
  waiting for transfers between devices: 208 us -> 0 us
  blocking collectives: 188 us -> 0 us
  Pallas kernels: 0 us -> 142 us
  other arithmetic: 80.3 us -> 0 us
  matrix products: 36.8 us -> 0 us
  between operations: 14.2 us -> 0.65 us
    psum x2 -> x0, waiting for transfers between devices: 208 us -> none  [the longest x1 142 us: on_device(): proto_back = lax.psum(proto_back, 'batch')]
    psum x6 -> x0, blocking collectives: 188 us -> none  [the longest x3 115 us: on_device(): row_weight = 1.0 / (tok_all * lax.psum(row_part, 'proto'))]
    pallas_call x0 -> x1, Pallas kernels: none -> 142 us  [on_device(): pl.pallas_call(functools.partial(kernel, nb, nq), out_shape=[jax.ShapeDty...]
    reduce_sum x11 -> x0, other arithmetic: 58.5 us -> none  [the longest x3 21.5 us: on_device(): row_part = jnp.sum(teach_exp * col_weight[None, :], axis=1)]
    dot_general x4 -> x0, matrix products: 36.8 us -> none  [the longest x2 18.5 us: similar(): lax.dot_general(left, right, (((1,), (1,)), ((), ())), preferred_element_...]
    convert_element_type x3 -> x0, other arithmetic: 21.6 us -> none  [the longest x1 12.3 us: on_device(): ((exp_logits / total[:, None] - targets) / (student_temp * tok_all)).asty...]
  transfers between devices with their start and end apart: 2 -> 0, of which waited for: 2 -> 0; matrix products, arithmetic and copies ran while one was open for 3% -> 0% of each run, Pallas kernels for 0% -> 0%
where the time goes in v2:
time: 149 us
  Pallas kernels  142 us (95%)
  local copies, waits for them, and re-layouts  6.92 us (5%)
    pallas_call x1, Pallas kernels, on_device(): pl.pallas_call(functools.partial(kernel, nb, nq), out_shape=[jax.ShapeDty...  142 us
    unnamed x4, local copies, waits for them, and re-layouts  6.92 us

profile of v2, /device:TPU:0, one launch (start us, length us, event | category | flops | bytes accessed | tf_op | source)
XLA Modules:
  0.0 149.3 jit_solution(15856716648099492024)
XLA Ops:
  0.6 141.7 %prototype_head.1 = (bf16[8192,384]{1,0:T(8,128)(2,1)}, bf16[512,384]{1,0:T(8,128)(2,1)}) custom-call(bf16[512,384]{1,0:T(8,128)(2,1)} %sf.1, bf16[512,384]{1,0:T(8,128)(2,1)} %tf.1, bf16[8192,384]{1,0:T(8,128)(2,1)} %sp_hbm.1, bf16[8192,384]{1,0:T(8,128)(2,1)} %tp_hbm.1), custom_call_target="tpu_custom_call" | custom-call | tf_op jit(solution)/shard_map/prototype_head/pallas_call | solution.py:503
  142.4 0.0 copy-start
  142.4 6.2 %copy.8 = bf16[8192,384]{1,0:T(8,128)(2,1)} copy(bf16[8192,384]{1,0:T(8,128)(2,1)} %get-tuple-element.4) | data formatting | bytes 12582912
  148.6 0.0 copy-done
  148.6 0.7 copy.9
Async XLA Ops:
  142.4 6.2 %copy-start = (bf16[512,384]{1,0:T(8,128)(2,1)S(1)}, bf16[512,384]{1,0:T(8,128)(2,1)}, u32[]{:S(2)}) copy-start(bf16[512,384]{1,0:T(8,128)(2,1)} %get-tuple-element.5) | copy-start | bytes 1179652

commit v3 on v2

v3 whole, which is shorter than its diff:
```python
import functools

import jax
import jax.numpy as jnp
from jax import lax
from jax.experimental import pallas as pl
from jax.experimental.pallas import tpu as pltpu
from jax.sharding import PartitionSpec as P

ITERS = 3
eps = 1e-06
teacher_temp = 0.04
student_temp = 0.1
LOG2E = 1.4426950408889634
F32 = jnp.float32
BF = jnp.bfloat16
MESH = pl.DeviceIdType.MESH
CH = 128


def nt(left, right):
    return lax.dot_general(
        left, right, (((1,), (1,)), ((), ())), preferred_element_type=F32
    )


def nn(left, right):
    return jnp.dot(left, right, preferred_element_type=F32)


def tn(left, right):
    return lax.dot_general(
        left, right, (((0,), (0,)), ((), ())), preferred_element_type=F32
    )


def loop(count, body):
    def step(i, carry):
        body(i)
        return carry

    lax.fori_loop(0, count, step, 0)


def rows(start, size):
    return pl.ds(pl.multiple_of(start, size), size)


def unit_rows(values):
    values = values.astype(F32)
    scale = lax.rsqrt(jnp.sum(values * values, axis=1, keepdims=True) + eps)
    return values * scale, scale


def back_norm(grad, unit, scale):
    return scale * (grad - unit * jnp.sum(grad * unit, axis=1, keepdims=True))


def kernel(
    nb, nq,
    sf_hbm, tf_hbm, sp_hbm, tp_hbm,
    gp_out, gs_out,
    sf, tf, t_all, s_all, sp, anchor, pu, e, s, cs, tot, fa, fb, ra, rb, st, ccol,
    r16, c16, w_src, w_mid, w_g1, w_g2, w_out, cx, yzr, sumf, xs, xr,
    lsem, tok_s, tok_r, fwd_s, fwd_r, spr_s, spr_r,
    a1_s, a1_r, a2_s, a2_r, g_s, g_r, f_s, f_r, sib_s, sib_r,
    ra_s, ra_r, rb_s, rb_r, yz_s, yz_r, xr_s, xr_r, gs_s, gs_r,
):
    nx = nb // 2
    far_dx = nx // 2
    tl, depth = sf.shape
    tokens = tl * nb
    pl_rows = sp.shape[0]
    protos = pl_rows * nb * nq
    chunks = pl_rows // CH
    wide = tokens // 128
    piece = tl // nq
    plane = 2 * tl
    b, p = lax.axis_index("batch"), lax.axis_index("proto")
    x, c = b // 2, lax.rem(b, 2)

    def bat(dx, dc):
        return lax.rem(x + dx, nx) * 2 + lax.rem(c + dc, 2)

    def peer(j):
        return (b, lax.rem(p + j, nq))

    def remote(src, dst, ss, rs, to):
        return pltpu.make_async_remote_copy(
            src, dst, ss, rs, device_id=to, device_id_type=MESH
        )

    sibling = (bat(0, 1), p)

    barrier = pltpu.get_barrier_semaphore()
    for j in range(1, nb):
        pl.semaphore_signal(
            barrier, inc=1, device_id=(lax.rem(b + j, nb), p), device_id_type=MESH
        )
    for j in range(1, nq):
        pl.semaphore_signal(barrier, inc=1, device_id=peer(j), device_id_type=MESH)
    mine = rows(b * pl_rows, pl_rows)
    loads = [
        pltpu.make_async_copy(tf_hbm, tf, lsem.at[0]),
        pltpu.make_async_copy(sf_hbm, sf, lsem.at[1]),
        pltpu.make_async_copy(tp_hbm.at[mine], anchor, lsem.at[2]),
        pltpu.make_async_copy(sp_hbm.at[mine], sp, lsem.at[3]),
    ]
    for d in loads:
        d.start()

    def norm_into(src, dst, start, count):
        def body(i):
            unit, _ = unit_rows(src[rows(i * 128, 128), :])
            dst[rows(start + i * 128, 128), :] = unit.astype(BF)

        loop(count // 128, body)

    loads[0].wait()
    norm_into(tf, t_all, b * tl, tl)
    pl.semaphore_wait(barrier, nb + nq - 2)

    feats = (t_all, s_all)

    def token_copy(f, dx):
        start, size = b * tl, tl
        if dx == far_dx:
            start, size = b * tl + p * piece, piece
        part = feats[f].at[rows(start, size)]
        to = sibling if dx == 0 else (bat(dx, 0), p)
        return remote(part, part, tok_s.at[f, dx], tok_r.at[f, dx], to)

    def spread(f, j):
        part = feats[f].at[rows(bat(nx - far_dx, 0) * tl + p * piece, piece)]
        return remote(part, part, spr_s.at[f, j - 1], spr_r.at[f, j - 1], peer(j))

    def forward(f, dx):
        block = feats[f].at[rows(bat(nx - dx, 0) * tl, tl)]
        return remote(block, block, fwd_s.at[f, dx], fwd_r.at[f, dx], sibling)

    near = (1, nx - 1)

    def tokens_send(f):
        for dx in (far_dx, 0) + near:
            token_copy(f, dx).start()

    def spread_start(f):
        token_copy(f, far_dx).wait_recv()
        for j in range(1, nq):
            spread(f, j).start()

    def spread_end(f):
        for j in range(1, nq):
            spread(f, j).wait_recv()
        forward(f, far_dx).start()

    def near_end(f):
        for dx in near:
            token_copy(f, dx).wait_recv()
            forward(f, dx).start()

    def tokens_drain(f):
        for dx in (far_dx, 0) + (() if f == 0 else near):
            token_copy(f, dx).wait_send()
        for dx in range(1, nx):
            forward(f, dx).wait_send()
        for j in range(1, nq):
            spread(f, j).wait_send()

    tokens_send(0)
    loads[2].wait()
    norm_into(anchor, anchor, 0, pl_rows)

    def exp_plane(left, right, out, dx, factor, accumulate):
        cols = rows(lax.rem(x + nx - dx, nx) * plane, plane)

        def body(i):
            sl = rows(i * 256, 256)
            value = jnp.exp2(nt(left[sl, :], right[cols, :]) * factor)
            out[sl, cols] = value.astype(BF)
            accumulate(value, sl, cols, dx)

        loop(pl_rows // 256, body)

    def col_acc(value, sl, cols, dx):
        acc = value[:, 0:128]
        for q in range(1, plane // 128):
            acc = acc + value[:, q * 128 : (q + 1) * 128]
        if dx == 0:
            cs[sl, :] = acc
        else:
            cs[sl, :] += acc

    def row_acc(value, sl, cols, dx):
        tot[:, cols] += jnp.sum(value.reshape(32, 8, plane), axis=0)

    def teacher_plane(dx):
        if dx:
            forward(0, dx).wait_recv()
        else:
            token_copy(0, 0).wait_recv()
        exp_plane(anchor, t_all, e, dx, LOG2E / teacher_temp, col_acc)

    def student_plane(dx):
        if dx:
            forward(1, dx).wait_recv()
        else:
            token_copy(1, 0).wait_recv()
        exp_plane(pu, s_all, s, dx, LOG2E / student_temp, row_acc)

    loads[1].wait()
    norm_into(sf, s_all, b * tl, tl)
    teacher_plane(0)
    spread_start(0)
    loads[3].wait()
    norm_into(sp, pu, 0, pl_rows)
    tot[...] = jnp.zeros_like(tot)
    for dx in near:
        token_copy(0, dx).wait_send()
    tokens_send(1)
    spread_end(0)
    near_end(0)
    teacher_plane(far_dx)
    teacher_plane(near[0])
    spread_start(1)
    teacher_plane(near[1])
    half = lax.broadcasted_iota(jnp.int32, (16, 128), 0) < 8

    def split_into(dst, j, row):
        high = row.astype(BF).astype(F32)
        dst[:, j * 128 : (j + 1) * 128] = jnp.where(half, high, row - high).astype(BF)

    def reduce_start(n, height):
        h = slice(0, height)
        ds = [
            remote(w_src.at[n, h], w_g1.at[n, j - 1, h], a1_s.at[n, j - 1],
                   a1_r.at[n, j - 1], (lax.rem(b + j, nb), p))
            for j in range(1, nb)
        ]
        for d in ds:
            d.start()
        return ds

    def reduce_middle(n, height, ds):
        h = slice(0, height)
        for d in ds:
            d.wait_recv()
        value = w_src[n, h]
        for j in range(nb - 1):
            value = value + w_g1[n, j, h]
        w_mid[n, h] = value
        out = [
            remote(w_mid.at[n, h], w_g2.at[n, j - 1, h], a2_s.at[n, j - 1],
                   a2_r.at[n, j - 1], peer(j))
            for j in range(1, nq)
        ]
        for d in out:
            d.start()
        return out

    def reduce_end(n, height, ds):
        h = slice(0, height)
        for d in ds:
            d.wait_recv()
        value = w_mid[n, h]
        for j in range(nq - 1):
            value = value + w_g2[n, j, h]
        return value

    def row_pass(n):
        out = nn(c16[...], e[...])
        line = out[0:1, :] + out[8:9, :]
        for j in range(wide):
            w_src[n, j : j + 1, :] = line[:, j * 128 : (j + 1) * 128]

    def col_pass(weights):
        for j in range(wide):
            split_into(r16, j, weights[j : j + 1, :])
        out = nt(r16[...], e[...])
        line = 1.0 / (protos * (out[0:1, :] + out[8:9, :]))
        return [line[:, j * 128 : (j + 1) * 128] for j in range(pl_rows // 128)]

    def feat_out(left, right, buf, base, to, ss, rs):
        def body(xx):
            cols = rows((xx * 2 + 1 - c) * tl, tl)
            sl = rows(base + xx * tl, tl)
            buf[sl, :] = tn(left[:, cols], right[...]).astype(BF)
            feat_copy(buf, base, to, ss, rs, xx).start()

        loop(nx, body)

    def feat_copy(buf, base, to, ss, rs, xx):
        return remote(
            buf.at[rows(base + xx * tl, tl)], to.at[rows(xx * tl, tl)],
            ss.at[xx], rs.at[xx], sibling,
        )

    def feat_own(left, right, out):
        def body(xx):
            cols = rows((xx * 2 + c) * tl, tl)
            out[rows(xx * tl, tl), :] = tn(left[:, cols], right[...])

        loop(nx, body)

    pending = []
    for j in range(pl_rows // 128):
        sums = jnp.sum(cs[j * 128 : (j + 1) * 128, :].T, axis=0, keepdims=True)
        split_into(c16, j, 1.0 / (protos * sums))
    row_pass(0)
    ds = reduce_start(0, wide)
    pending += ds
    student_plane(0)
    spread_end(1)
    ds = reduce_middle(0, wide, ds)
    pending += ds
    student_plane(far_dx)
    near_end(1)
    student_plane(near[0])
    student_plane(near[1])
    tokens_drain(0)
    weights = 1.0 / (tokens * reduce_end(0, wide, ds))
    for j, line in enumerate(col_pass(weights)):
        split_into(c16, j, line)
    row_pass(1)
    line = jnp.sum(tot[...], axis=0, keepdims=True)
    for j in range(wide):
        w_src[1, wide + j : wide + j + 1, :] = line[:, j * 128 : (j + 1) * 128]
    ds = reduce_start(1, 2 * wide)
    pending += ds
    feat_out(s, pu, t_all, 0, ra, ra_s, ra_r)
    ds = reduce_middle(1, 2 * wide, ds)
    pending += ds
    feat_own(s, pu, fa)
    value = reduce_end(1, 2 * wide, ds)
    weights = 1.0 / (tokens * value[0:wide])
    w_out[wide : 2 * wide, :] = 1.0 / (student_temp * tokens * value[wide : 2 * wide])
    lines = col_pass(weights)
    for j, line in enumerate(lines):
        split_into(c16, j, line)
    row_pass(2)
    ds = reduce_start(2, wide)
    pending += ds
    for j, line in enumerate(lines):
        ccol[j * 128 : (j + 1) * 128, :] = jnp.broadcast_to(line, (128, 128)).T

    def scale_protos(j):
        sl = rows(j * 128, 128)
        anchor[sl, :] = (ccol[sl, 0:1] * pu[sl, :].astype(F32)).astype(BF)

    loop(pl_rows // 128, scale_protos)
    feat_out(e, anchor, t_all, nx * tl, rb, rb_s, rb_r)
    ds = reduce_middle(2, wide, ds)
    pending += ds
    feat_own(e, anchor, fb)

    def column(j):
        return jnp.broadcast_to(w_out[pl.ds(j, 1), :], (128, 128)).T[:, 0:1]

    def student_weights(j):
        sl = rows(j * 128, 128)
        st[sl, :] = (s_all[sl, :].astype(F32) * column(wide + j)).astype(BF)

    loop(wide, student_weights)
    tokens_drain(1)
    for xx in range(nx):
        feat_copy(t_all, 0, ra, ra_s, ra_r, xx).wait()
        feat_copy(t_all, nx * tl, rb, rb_s, rb_r, xx).wait()
    w_out[0:wide, :] = (1.0 / student_temp) / (tokens * reduce_end(2, wide, ds))

    group = tl // 128

    def combine(i):
        sl = rows(i * 128, 128)
        j = ((i // group) * 2 + c) * group + lax.rem(i, group)
        value = (fa[sl, :] + ra[sl, :].astype(F32)) * column(wide + j)
        value = value - (fb[sl, :] + rb[sl, :].astype(F32)) * column(j)
        cx[i // group, rows(lax.rem(i, group) * 128, 128), :] = value.astype(BF)

    loop(nx * group, combine)
    yz_d = []
    for j in range(1, nq):
        d = remote(
            cx.at[:, rows(lax.rem(p + j, nq) * piece, piece), :], yzr.at[j - 1],
            yz_s.at[j - 1], yz_r.at[j - 1], peer(j),
        )
        d.start()
        yz_d.append(d)

    def teacher_weights(j):
        sl = rows(j * 128, 128)
        s_all[sl, :] = (s_all[sl, :].astype(F32) * column(j)).astype(BF)

    loop(wide, teacher_weights)

    def chunk_part(block, q):
        return gp_out.at[rows(block * pl_rows + q * CH, CH)]

    def chunk_send(q, k):
        to = (bat(1, 0), p) if k == 0 else (bat(nx - 1, 0), p)
        part = chunk_part(b, q)
        return remote(part, part, g_s.at[k, q], g_r.at[k, q], to)

    def chunk_forward(q, k):
        block = bat(nx - 1, 0) if k == 0 else bat(1, 0)
        to = (bat(1, 0), p) if k == 0 else (bat(nx - 1, 0), p)
        size = CH // 2
        part = gp_out.at[rows(block * pl_rows + q * CH + k * size, size)]
        return remote(part, part, f_s.at[k, q], f_r.at[k, q], to)

    def chunk_sibling(q, k):
        part = chunk_part(bat((0, nx - 1, 1, 2)[k], 0), q)
        return remote(part, part, sib_s.at[k, q], sib_r.at[k, q], sibling)

    def chunk_compute(q):
        sl = rows(q * CH, CH)
        back = nn(s[sl, :], st[...]) - ccol[sl, 0:1] * nn(e[sl, :], s_all[...])
        unit, scale = unit_rows(sp[sl, :])
        value = back_norm(back, unit, scale).astype(BF)
        gp_out[rows(b * pl_rows + q * CH, CH), :] = value
        chunk_send(q, 0).start()
        chunk_send(q, 1).start()
        chunk_sibling(q, 0).start()

    def chunk_recv(q):
        for k in range(2):
            chunk_send(q, k).wait_recv()
            chunk_forward(q, k).start()
            chunk_sibling(q, 1 + k).start()

    def chunk_last(q):
        for k in range(2):
            chunk_forward(q, k).wait_recv()
        chunk_sibling(q, 3).start()

    lag = 3
    loop(lag, chunk_compute)

    def chunk_both(q):
        chunk_compute(q + lag)
        chunk_recv(q)

    loop(chunks - lag, chunk_both)
    loop(lag, lambda q: chunk_recv(q + chunks - lag))
    for d in yz_d:
        d.wait_recv()
    value = cx[:, rows(p * piece, piece), :].astype(F32)
    for j in range(nq - 1):
        value = value + yzr[j].astype(F32)
    sumf[...] = value
    xs[...] = value.astype(BF)
    xr_d = []
    for dx in range(1, nx):
        d = remote(
            xs.at[lax.rem(x + dx, nx)], xr.at[dx - 1],
            xr_s.at[dx - 1], xr_r.at[dx - 1], (bat(dx, 0), p),
        )
        d.start()
        xr_d.append(d)
    loop(chunks, chunk_last)
    for d in xr_d:
        d.wait_recv()
    value = sumf[x]
    for dx in range(nx - 1):
        value = value + xr[dx].astype(F32)
    own = rows(p * piece, piece)
    unit, scale = unit_rows(sf[own, :])
    gs_out[own, :] = back_norm(value, unit, scale).astype(BF)
    gs_d = []
    for j in range(1, nq):
        part = gs_out.at[own]
        d = remote(part, part, gs_s.at[j - 1], gs_r.at[j - 1], peer(j))
        d.start()
        gs_d.append(d)

    for d in pending + yz_d + xr_d + gs_d:
        d.wait_send()

    def drain(q):
        for k in range(2):
            chunk_send(q, k).wait_send()
            chunk_forward(q, k).wait_send()
        for k in range(4):
            chunk_sibling(q, k).wait()

    loop(chunks, drain)
    for d in gs_d:
        d.wait_recv()


def on_device(nb, nq, student_feats, teacher_feats, student_protos, teacher_protos):
    tl, depth = student_feats.shape
    pl_rows = student_protos.shape[0] // nb
    tokens = tl * nb
    chunks = pl_rows // CH
    wide = tokens // 128
    nx = nb // 2
    piece = tl // nq
    vm = pltpu.VMEM
    dma = pltpu.SemaphoreType.DMA
    half = tokens // 2
    scratch = [
        vm((tl, depth), BF),
        vm((tl, depth), BF),
        vm((tokens, depth), BF),
        vm((tokens, depth), BF),
        vm((pl_rows, depth), BF),
        vm((pl_rows, depth), BF),
        vm((pl_rows, depth), BF),
        vm((pl_rows, tokens), BF),
        vm((pl_rows, tokens), BF),
        vm((pl_rows, 128), F32),
        vm((8, tokens), F32),
        vm((half, depth), F32),
        vm((half, depth), F32),
        vm((half, depth), BF),
        vm((half, depth), BF),
        vm((tokens, depth), BF),
        vm((pl_rows, 128), F32),
        vm((16, tokens), BF),
        vm((16, pl_rows), BF),
        vm((ITERS, 2 * wide, 128), F32),
        vm((ITERS, 2 * wide, 128), F32),
        vm((ITERS, nb - 1, 2 * wide, 128), F32),
        vm((ITERS, nq - 1, 2 * wide, 128), F32),
        vm((2 * wide, 128), F32),
        vm((nx, tl, depth), BF),
        vm((nq - 1, nx, piece, depth), BF),
        vm((nx, piece, depth), F32),
        vm((nx, piece, depth), BF),
        vm((nx - 1, piece, depth), BF),
        dma((4,)),
        dma((2, nx)), dma((2, nx)), dma((2, nx)), dma((2, nx)),
        dma((2, nq - 1)), dma((2, nq - 1)),
        dma((ITERS, nb - 1)), dma((ITERS, nb - 1)),
        dma((ITERS, nq - 1)), dma((ITERS, nq - 1)),
        dma((2, chunks)), dma((2, chunks)), dma((2, chunks)), dma((2, chunks)),
        dma((4, chunks)), dma((4, chunks)),
        dma((nx,)), dma((nx,)), dma((nx,)), dma((nx,)),
        dma((nq - 1,)), dma((nq - 1,)),
        dma((nx - 1,)), dma((nx - 1,)),
        dma((nq - 1,)), dma((nq - 1,)),
    ]
    in_vmem = pl.BlockSpec(memory_space=pltpu.VMEM)
    anywhere = pl.BlockSpec(memory_space=pl.ANY)
    return pl.pallas_call(
        functools.partial(kernel, nb, nq),
        out_shape=[
            pltpu.VMEM(student_protos.shape, BF),
            pltpu.VMEM(student_feats.shape, BF),
        ],
        in_specs=[anywhere] * 4,
        out_specs=[in_vmem, in_vmem],
        scratch_shapes=scratch,
        compiler_params=pltpu.CompilerParams(
            collective_id=0, has_side_effects=True, vmem_limit_bytes=54 << 20
        ),
        name="prototype_head",
    )(student_feats, teacher_feats, student_protos, teacher_protos)


def solution(mesh):
    nb, nq = mesh.shape["batch"], mesh.shape["proto"]
    in_specs = (P("batch", None), P("batch", None), P("proto", None), P("proto", None))
    out_specs = (P("proto", None), P("batch", None))
    return jax.shard_map(
        functools.partial(on_device, nb, nq),
        mesh=mesh, in_specs=in_specs, out_specs=out_specs, check_vma=False,
    )
```

time: 149 us -> 130 us (0.87)
  Pallas kernels: 142 us -> 126 us
  local copies, waits for them, and re-layouts: 6.92 us -> 3.45 us
    pallas_call x1, Pallas kernels: 142 us -> 126 us  [on_device(): pl.pallas_call(functools.partial(kernel, nb, nq), out_shape=[pltpu.VMEM(s...]
    unnamed x4 -> x2, local copies, waits for them, and re-layouts: 6.92 us -> 3.45 us
where the time goes in v3:
time: 130 us
  Pallas kernels  126 us (97%)
  local copies, waits for them, and re-layouts  3.45 us (3%)
    pallas_call x1, Pallas kernels, on_device(): pl.pallas_call(functools.partial(kernel, nb, nq), out_shape=[pltpu.VMEM(s...  126 us
    unnamed x2, local copies, waits for them, and re-layouts  3.45 us

profile of v3, /device:TPU:0, one launch (start us, length us, event | category | flops | bytes accessed | tf_op | source)
XLA Modules:
  0.0 129.9 jit_solution(7629043801045402834)
XLA Ops:
  0.6 125.8 %prototype_head.1 = (bf16[8192,384]{1,0:T(8,128)(2,1)S(1)}, bf16[512,384]{1,0:T(8,128)(2,1)S(1)}) custom-call(bf16[512,384]{1,0:T(8,128)(2,1)} %sf_hbm.1, bf16[512,384]{1,0:T(8,128)(2,1)} %tf_hbm.1, bf16[8192,384]{1,0:T(8,128)(2,1)} %sp_hbm.1, bf16[8192,384]{1,0:T(8,128)(2,1)} %tp_hbm.1), custom_call_target="tpu_custom_call" | custom-call | tf_op jit(solution)/shard_map/prototype_head/pallas_call | solution.py:545
  126.5 2.7 %copy.8 = bf16[8192,384]{1,0:T(8,128)(2,1)} copy(bf16[8192,384]{1,0:T(8,128)(2,1)S(1)} %get-tuple-element.2) | data formatting | bytes 12582912
  129.2 0.7 copy.9

commit v4 on v3

--- a/solution.py
+++ b/solution.py
@@ -16,6 +16,7 @@
 BF = jnp.bfloat16
 MESH = pl.DeviceIdType.MESH
 CH = 128
+NZ = 4
 
 
 def nt(left, right):
@@ -61,13 +62,16 @@
     sf_hbm, tf_hbm, sp_hbm, tp_hbm,
     gp_out, gs_out,
     sf, tf, t_all, s_all, sp, anchor, pu, e, s, cs, tot, fa, fb, ra, rb, st, ccol,
-    r16, c16, w_src, w_mid, w_g1, w_g2, w_out, cx, yzr, sumf, xs, xr,
+    r16, c16, w_src, w_mid, w_g1, w_g2, w_out, cx, b1y, b1z, c2y, c2z, b2y, b2z, sumf, xs, xr,
     lsem, tok_s, tok_r, fwd_s, fwd_r, spr_s, spr_r,
     a1_s, a1_r, a2_s, a2_r, g_s, g_r, f_s, f_r, sib_s, sib_r,
-    ra_s, ra_r, rb_s, rb_r, yz_s, yz_r, xr_s, xr_r, gs_s, gs_r,
+    ra_s, ra_r, rb_s, rb_r, y1_s, y1_r, z1_s, z1_r, y2_s, y2_r, z2_s, z2_r, xr_s, xr_r, gs_s, gs_r,
 ):
     nx = nb // 2
     far_dx = nx // 2
+    hx = nx // 2
+    nz = NZ
+    ny = nq // nz
     tl, depth = sf.shape
     tokens = tl * nb
     pl_rows = sp.shape[0]
@@ -78,6 +82,7 @@
     plane = 2 * tl
     b, p = lax.axis_index("batch"), lax.axis_index("proto")
     x, c = b // 2, lax.rem(b, 2)
+    y, z = p // nz, lax.rem(p, nz)
 
     def bat(dx, dc):
         return lax.rem(x + dx, nx) * 2 + lax.rem(c + dc, 2)
@@ -230,41 +235,40 @@
         high = row.astype(BF).astype(F32)
         dst[:, j * 128 : (j + 1) * 128] = jnp.where(half, high, row - high).astype(BF)
 
-    def reduce_start(n, height):
-        h = slice(0, height)
+    def reduce_start(n):
         ds = [
-            remote(w_src.at[n, h], w_g1.at[n, j - 1, h], a1_s.at[n, j - 1],
+            remote(w_src.at[n], w_g1.at[n, j - 1], a1_s.at[n, j - 1],
                    a1_r.at[n, j - 1], (lax.rem(b + j, nb), p))
             for j in range(1, nb)
         ]
         for d in ds:
             d.start()
+        pending.extend(ds)
         return ds
 
-    def reduce_middle(n, height, ds):
-        h = slice(0, height)
+    def reduce_middle(n, ds):
         for d in ds:
             d.wait_recv()
-        value = w_src[n, h]
+        value = w_src[n]
         for j in range(nb - 1):
-            value = value + w_g1[n, j, h]
-        w_mid[n, h] = value
-        out = [
-            remote(w_mid.at[n, h], w_g2.at[n, j - 1, h], a2_s.at[n, j - 1],
+            value = value + w_g1[n, j]
+        w_mid[n] = value.astype(BF)
+        ds = [
+            remote(w_mid.at[n], w_g2.at[n, j - 1], a2_s.at[n, j - 1],
                    a2_r.at[n, j - 1], peer(j))
             for j in range(1, nq)
         ]
-        for d in out:
+        for d in ds:
             d.start()
-        return out
-
-    def reduce_end(n, height, ds):
-        h = slice(0, height)
+        pending.extend(ds)
+        return ds
+
+    def reduce_end(n, ds):
         for d in ds:
             d.wait_recv()
-        value = w_mid[n, h]
+        value = w_mid[n].astype(F32)
         for j in range(nq - 1):
-            value = value + w_g2[n, j, h]
+            value = value + w_g2[n, j].astype(F32)
         return value
 
     def row_pass(n):
@@ -307,39 +311,34 @@
         sums = jnp.sum(cs[j * 128 : (j + 1) * 128, :].T, axis=0, keepdims=True)
         split_into(c16, j, 1.0 / (protos * sums))
     row_pass(0)
-    ds = reduce_start(0, wide)
-    pending += ds
+    ds = reduce_start(0)
     student_plane(0)
     spread_end(1)
-    ds = reduce_middle(0, wide, ds)
-    pending += ds
+    ds = reduce_middle(0, ds)
     student_plane(far_dx)
     near_end(1)
     student_plane(near[0])
     student_plane(near[1])
     tokens_drain(0)
-    weights = 1.0 / (tokens * reduce_end(0, wide, ds))
+    weights = 1.0 / (tokens * reduce_end(0, ds))
     for j, line in enumerate(col_pass(weights)):
         split_into(c16, j, line)
     row_pass(1)
+    ds = reduce_start(1)
     line = jnp.sum(tot[...], axis=0, keepdims=True)
     for j in range(wide):
-        w_src[1, wide + j : wide + j + 1, :] = line[:, j * 128 : (j + 1) * 128]
-    ds = reduce_start(1, 2 * wide)
-    pending += ds
+        w_src[ITERS, j : j + 1, :] = line[:, j * 128 : (j + 1) * 128]
+    dt = reduce_start(ITERS)
     feat_out(s, pu, t_all, 0, ra, ra_s, ra_r)
-    ds = reduce_middle(1, 2 * wide, ds)
-    pending += ds
+    ds = reduce_middle(1, ds)
+    dt = reduce_middle(ITERS, dt)
     feat_own(s, pu, fa)
-    value = reduce_end(1, 2 * wide, ds)
-    weights = 1.0 / (tokens * value[0:wide])
-    w_out[wide : 2 * wide, :] = 1.0 / (student_temp * tokens * value[wide : 2 * wide])
+    weights = 1.0 / (tokens * reduce_end(1, ds))
     lines = col_pass(weights)
     for j, line in enumerate(lines):
         split_into(c16, j, line)
     row_pass(2)
-    ds = reduce_start(2, wide)
-    pending += ds
+    ds = reduce_start(2)
     for j, line in enumerate(lines):
         ccol[j * 128 : (j + 1) * 128, :] = jnp.broadcast_to(line, (128, 128)).T
 
@@ -349,8 +348,8 @@
 
     loop(pl_rows // 128, scale_protos)
     feat_out(e, anchor, t_all, nx * tl, rb, rb_s, rb_r)
-    ds = reduce_middle(2, wide, ds)
-    pending += ds
+    ds = reduce_middle(2, ds)
+    w_out[wide : 2 * wide, :] = 1.0 / (student_temp * tokens * reduce_end(ITERS, dt))
     feat_own(e, anchor, fb)
 
     def column(j):
@@ -365,7 +364,7 @@
     for xx in range(nx):
         feat_copy(t_all, 0, ra, ra_s, ra_r, xx).wait()
         feat_copy(t_all, nx * tl, rb, rb_s, rb_r, xx).wait()
-    w_out[0:wide, :] = (1.0 / student_temp) / (tokens * reduce_end(2, wide, ds))
+    w_out[0:wide, :] = (1.0 / student_temp) / (tokens * reduce_end(2, ds))
 
     group = tl // 128
 
@@ -374,17 +373,88 @@
         j = ((i // group) * 2 + c) * group + lax.rem(i, group)
         value = (fa[sl, :] + ra[sl, :].astype(F32)) * column(wide + j)
         value = value - (fb[sl, :] + rb[sl, :].astype(F32)) * column(j)
-        cx[i // group, rows(lax.rem(i, group) * 128, 128), :] = value.astype(BF)
+        cx[i // group, lax.rem(i, group)] = value.astype(BF).reshape(nz, piece, depth)
 
     loop(nx * group, combine)
-    yz_d = []
-    for j in range(1, nq):
-        d = remote(
-            cx.at[:, rows(lax.rem(p + j, nq) * piece, piece), :], yzr.at[j - 1],
-            yz_s.at[j - 1], yz_r.at[j - 1], peer(j),
-        )
+    feat_d = []
+
+    def feat_send(src, dst, ss, rs, to):
+        d = remote(src, dst, ss, rs, to)
         d.start()
-        yz_d.append(d)
+        feat_d.append(d)
+        return d
+
+    def along_y(d):
+        return lax.rem(y + d, ny)
+
+    def along_z(d):
+        return lax.rem(z + d, nz)
+
+    first = [
+        feat_send(cx.at[0:hx, along_y(d)], b1y.at[d - 1], y1_s.at[d - 1],
+                  y1_r.at[d - 1], (b, along_y(d) * nz + z))
+        for d in range(1, ny)
+    ] + [
+        feat_send(cx.at[hx:nx, :, along_z(d)], b1z.at[d - 1], z1_s.at[d - 1],
+                  z1_r.at[d - 1], (b, y * nz + along_z(d)))
+        for d in range(1, nz)
+    ]
+
+    def feat_middle():
+        for d in first:
+            d.wait_recv()
+        for h in range(hx):
+            value = cx[h, y].astype(F32)
+            for d in range(ny - 1):
+                value = value + b1y[d, h].astype(F32)
+            c2y[h] = value.astype(BF)
+            value = cx[hx + h, :, z].astype(F32)
+            for d in range(nz - 1):
+                value = value + b1z[d, h].astype(F32)
+            c2z[h] = value.astype(BF)
+        return [
+            feat_send(c2y.at[:, along_z(d)], b2y.at[d - 1], z2_s.at[d - 1],
+                      z2_r.at[d - 1], (b, y * nz + along_z(d)))
+            for d in range(1, nz)
+        ] + [
+            feat_send(c2z.at[:, along_y(d)], b2z.at[d - 1], y2_s.at[d - 1],
+                      y2_r.at[d - 1], (b, along_y(d) * nz + z))
+            for d in range(1, ny)
+        ]
+
+    def feat_x(second):
+        for d in second:
+            d.wait_recv()
+        value = c2y[:, z].astype(F32)
+        for d in range(nz - 1):
+            value = value + b2y[d].astype(F32)
+        sumf[0:hx] = value
+        xs[0:hx] = value.astype(BF)
+        value = c2z[:, y].astype(F32)
+        for d in range(ny - 1):
+            value = value + b2z[d].astype(F32)
+        sumf[hx:nx] = value
+        xs[hx:nx] = value.astype(BF)
+        return [
+            feat_send(xs.at[lax.rem(x + dx, nx)], xr.at[dx - 1],
+                      xr_s.at[dx - 1], xr_r.at[dx - 1], (bat(dx, 0), p))
+            for dx in range(1, nx)
+        ]
+
+    def feat_last(third):
+        for d in third:
+            d.wait_recv()
+        value = sumf[x]
+        for dx in range(nx - 1):
+            value = value + xr[dx].astype(F32)
+        own = rows(p * piece, piece)
+        unit, scale = unit_rows(sf[own, :])
+        gs_out[own, :] = back_norm(value, unit, scale).astype(BF)
+        part = gs_out.at[own]
+        return [
+            feat_send(part, part, gs_s.at[j - 1], gs_r.at[j - 1], peer(j))
+            for j in range(1, nq)
+        ]
 
     def teacher_weights(j):
         sl = rows(j * 128, 128)
@@ -439,40 +509,16 @@
         chunk_compute(q + lag)
         chunk_recv(q)
 
-    loop(chunks - lag, chunk_both)
-    loop(lag, lambda q: chunk_recv(q + chunks - lag))
-    for d in yz_d:
-        d.wait_recv()
-    value = cx[:, rows(p * piece, piece), :].astype(F32)
-    for j in range(nq - 1):
-        value = value + yzr[j].astype(F32)
-    sumf[...] = value
-    xs[...] = value.astype(BF)
-    xr_d = []
-    for dx in range(1, nx):
-        d = remote(
-            xs.at[lax.rem(x + dx, nx)], xr.at[dx - 1],
-            xr_s.at[dx - 1], xr_r.at[dx - 1], (bat(dx, 0), p),
-        )
-        d.start()
-        xr_d.append(d)
+    loop(2, chunk_both)
+    second = feat_middle()
+    loop(chunks - lag - 2, lambda q: chunk_both(q + 2))
+    third = feat_x(second)
+    chunk_recv(chunks - lag)
+    final = feat_last(third)
+    loop(lag - 1, lambda q: chunk_recv(q + chunks - lag + 1))
     loop(chunks, chunk_last)
-    for d in xr_d:
-        d.wait_recv()
-    value = sumf[x]
-    for dx in range(nx - 1):
-        value = value + xr[dx].astype(F32)
-    own = rows(p * piece, piece)
-    unit, scale = unit_rows(sf[own, :])
-    gs_out[own, :] = back_norm(value, unit, scale).astype(BF)
-    gs_d = []
-    for j in range(1, nq):
-        part = gs_out.at[own]
-        d = remote(part, part, gs_s.at[j - 1], gs_r.at[j - 1], peer(j))
-        d.start()
-        gs_d.append(d)
-
-    for d in pending + yz_d + xr_d + gs_d:
+
+    for d in pending + feat_d:
         d.wait_send()
 
     def drain(q):
@@ -483,7 +529,7 @@
             chunk_sibling(q, k).wait()
 
     loop(chunks, drain)
-    for d in gs_d:
+    for d in final:
         d.wait_recv()
 
 
@@ -498,6 +544,8 @@
     vm = pltpu.VMEM
     dma = pltpu.SemaphoreType.DMA
     half = tokens // 2
+    hx, nz = nx // 2, NZ
+    ny = nq // nz
     scratch = [
         vm((tl, depth), BF),
         vm((tl, depth), BF),
@@ -518,25 +566,31 @@
         vm((pl_rows, 128), F32),
         vm((16, tokens), BF),
         vm((16, pl_rows), BF),
-        vm((ITERS, 2 * wide, 128), F32),
-        vm((ITERS, 2 * wide, 128), F32),
-        vm((ITERS, nb - 1, 2 * wide, 128), F32),
-        vm((ITERS, nq - 1, 2 * wide, 128), F32),
+        vm((ITERS + 1, wide, 128), F32),
+        vm((ITERS + 1, wide, 128), BF),
+        vm((ITERS + 1, nb - 1, wide, 128), F32),
+        vm((ITERS + 1, nq - 1, wide, 128), BF),
         vm((2 * wide, 128), F32),
-        vm((nx, tl, depth), BF),
-        vm((nq - 1, nx, piece, depth), BF),
+        vm((nx, ny, nz, piece, depth), BF),
+        vm((ny - 1, hx, nz, piece, depth), BF),
+        vm((nz - 1, hx, ny, piece, depth), BF),
+        vm((hx, nz, piece, depth), BF),
+        vm((hx, ny, piece, depth), BF),
+        vm((nz - 1, hx, piece, depth), BF),
+        vm((ny - 1, hx, piece, depth), BF),
         vm((nx, piece, depth), F32),
         vm((nx, piece, depth), BF),
         vm((nx - 1, piece, depth), BF),
         dma((4,)),
         dma((2, nx)), dma((2, nx)), dma((2, nx)), dma((2, nx)),
         dma((2, nq - 1)), dma((2, nq - 1)),
-        dma((ITERS, nb - 1)), dma((ITERS, nb - 1)),
-        dma((ITERS, nq - 1)), dma((ITERS, nq - 1)),
+        dma((ITERS + 1, nb - 1)), dma((ITERS + 1, nb - 1)),
+        dma((ITERS + 1, nq - 1)), dma((ITERS + 1, nq - 1)),
         dma((2, chunks)), dma((2, chunks)), dma((2, chunks)), dma((2, chunks)),
         dma((4, chunks)), dma((4, chunks)),
         dma((nx,)), dma((nx,)), dma((nx,)), dma((nx,)),
-        dma((nq - 1,)), dma((nq - 1,)),
+        dma((ny - 1,)), dma((ny - 1,)), dma((nz - 1,)), dma((nz - 1,)),
+        dma((ny - 1,)), dma((ny - 1,)), dma((nz - 1,)), dma((nz - 1,)),
         dma((nx - 1,)), dma((nx - 1,)),
         dma((nq - 1,)), dma((nq - 1,)),
     ]

time: 130 us -> 122 us (0.938)
  Pallas kernels: 126 us -> 118 us
    pallas_call x1, Pallas kernels: 126 us -> 118 us  [on_device(): pl.pallas_call(functools.partial(kernel, nb, nq), out_shape=[pltpu.VMEM(s...]
where the time goes in v4:
time: 122 us
  Pallas kernels  118 us (97%)
  local copies, waits for them, and re-layouts  3.45 us (3%)
    pallas_call x1, Pallas kernels, on_device(): pl.pallas_call(functools.partial(kernel, nb, nq), out_shape=[pltpu.VMEM(s...  118 us
    unnamed x2, local copies, waits for them, and re-layouts  3.45 us

profile of v4, /device:TPU:0, one launch (start us, length us, event | category | flops | bytes accessed | tf_op | source)
XLA Modules:
  0.0 121.6 jit_solution(6688870198260885440)
XLA Ops:
  0.6 117.5 %prototype_head.1 = (bf16[8192,384]{1,0:T(8,128)(2,1)S(1)}, bf16[512,384]{1,0:T(8,128)(2,1)S(1)}) custom-call(bf16[512,384]{1,0:T(8,128)(2,1)} %sf_hbm.1, bf16[512,384]{1,0:T(8,128)(2,1)} %tf_hbm.1, bf16[8192,384]{1,0:T(8,128)(2,1)} %sp_hbm.1, bf16[8192,384]{1,0:T(8,128)(2,1)} %tp_hbm.1), custom_call_target="tpu_custom_call" | custom-call | tf_op jit(solution)/shard_map/prototype_head/pallas_call | solution.py:599
  118.1 2.7 %copy.8 = bf16[8192,384]{1,0:T(8,128)(2,1)} copy(bf16[8192,384]{1,0:T(8,128)(2,1)S(1)} %get-tuple-element.2) | data formatting | bytes 12582912
  120.9 0.7 copy.9

commit v5 on v4

--- a/solution.py
+++ b/solution.py
@@ -61,9 +61,9 @@
     nb, nq,
     sf_hbm, tf_hbm, sp_hbm, tp_hbm,
     gp_out, gs_out,
-    sf, tf, t_all, s_all, sp, anchor, pu, e, s, cs, tot, fa, fb, ra, rb, st, ccol,
+    sf, tf, t_all, s_all, sp, anchor, pu, e, s, cs, tot, fa, fb, ra, rb, oa, ob, put, anct, ccol,
     r16, c16, w_src, w_mid, w_g1, w_g2, w_out, cx, b1y, b1z, c2y, c2z, b2y, b2z, sumf, xs, xr,
-    lsem, tok_s, tok_r, fwd_s, fwd_r, spr_s, spr_r,
+    lsem, near_s, near_r, nfwd_s, nfwd_r, tok_s, tok_r, fwd_s, fwd_r, spr_s, spr_r,
     a1_s, a1_r, a2_s, a2_r, g_s, g_r, f_s, f_r, sib_s, sib_r,
     ra_s, ra_r, rb_s, rb_r, y1_s, y1_r, z1_s, z1_r, y2_s, y2_r, z2_s, z2_r, xr_s, xr_r, gs_s, gs_r,
 ):
@@ -127,6 +127,18 @@
 
     feats = (t_all, s_all)
 
+    def near_copy(f, dx, h):
+        part = feats[f].at[rows(b * tl + h * (tl // 2), tl // 2)]
+        return remote(
+            part, part, near_s.at[f, dx, h], near_r.at[f, dx, h], (bat(dx, 0), p)
+        )
+
+    def near_forward(f, dx, h):
+        part = feats[f].at[rows(bat(nx - dx, 0) * tl + h * (tl // 2), tl // 2)]
+        return remote(
+            part, part, nfwd_s.at[f, dx, h], nfwd_r.at[f, dx, h], sibling
+        )
+
     def token_copy(f, dx):
         start, size = b * tl, tl
         if dx == far_dx:
@@ -146,8 +158,11 @@
     near = (1, nx - 1)
 
     def tokens_send(f):
-        for dx in (far_dx, 0) + near:
-            token_copy(f, dx).start()
+        token_copy(f, far_dx).start()
+        token_copy(f, 0).start()
+        for h in range(2):
+            for dx in near:
+                near_copy(f, dx, h).start()
 
     def spread_start(f):
         token_copy(f, far_dx).wait_recv()
@@ -160,15 +175,20 @@
         forward(f, far_dx).start()
 
     def near_end(f):
-        for dx in near:
-            token_copy(f, dx).wait_recv()
-            forward(f, dx).start()
+        for h in range(2):
+            for dx in near:
+                near_copy(f, dx, h).wait_recv()
+                near_forward(f, dx, h).start()
 
     def tokens_drain(f):
-        for dx in (far_dx, 0) + (() if f == 0 else near):
-            token_copy(f, dx).wait_send()
-        for dx in range(1, nx):
-            forward(f, dx).wait_send()
+        token_copy(f, far_dx).wait_send()
+        token_copy(f, 0).wait_send()
+        forward(f, far_dx).wait_send()
+        for h in range(2):
+            for dx in near:
+                if f:
+                    near_copy(f, dx, h).wait_send()
+                near_forward(f, dx, h).wait_send()
         for j in range(1, nq):
             spread(f, j).wait_send()
 
@@ -200,15 +220,21 @@
         tot[:, cols] += jnp.sum(value.reshape(32, 8, plane), axis=0)
 
     def teacher_plane(dx):
-        if dx:
+        if dx == far_dx:
             forward(0, dx).wait_recv()
+        elif dx:
+            for h in range(2):
+                near_forward(0, dx, h).wait_recv()
         else:
             token_copy(0, 0).wait_recv()
         exp_plane(anchor, t_all, e, dx, LOG2E / teacher_temp, col_acc)
 
     def student_plane(dx):
-        if dx:
+        if dx == far_dx:
             forward(1, dx).wait_recv()
+        elif dx:
+            for h in range(2):
+                near_forward(1, dx, h).wait_recv()
         else:
             token_copy(1, 0).wait_recv()
         exp_plane(pu, s_all, s, dx, LOG2E / student_temp, row_acc)
@@ -218,10 +244,18 @@
     teacher_plane(0)
     spread_start(0)
     loads[3].wait()
-    norm_into(sp, pu, 0, pl_rows)
+
+    def norm_protos(i):
+        sl = rows(i * 128, 128)
+        unit, _ = unit_rows(sp[sl, :])
+        pu[sl, :] = unit.astype(BF)
+        put[:, sl] = unit.T.astype(BF)
+
+    loop(pl_rows // 128, norm_protos)
     tot[...] = jnp.zeros_like(tot)
-    for dx in near:
-        token_copy(0, dx).wait_send()
+    for h in range(2):
+        for dx in near:
+            near_copy(0, dx, h).wait_send()
     tokens_send(1)
     spread_end(0)
     near_end(0)
@@ -284,25 +318,21 @@
         line = 1.0 / (protos * (out[0:1, :] + out[8:9, :]))
         return [line[:, j * 128 : (j + 1) * 128] for j in range(pl_rows // 128)]
 
-    def feat_out(left, right, buf, base, to, ss, rs):
+    def feat_copy(buf, to, ss, rs, xx):
+        return remote(buf.at[xx], to.at[xx], ss.at[xx], rs.at[xx], sibling)
+
+    def feat_out(left, right, buf, to, ss, rs):
         def body(xx):
             cols = rows((xx * 2 + 1 - c) * tl, tl)
-            sl = rows(base + xx * tl, tl)
-            buf[sl, :] = tn(left[:, cols], right[...]).astype(BF)
-            feat_copy(buf, base, to, ss, rs, xx).start()
+            buf[xx] = nn(left[...], right[:, cols]).astype(BF)
+            feat_copy(buf, to, ss, rs, xx).start()
 
         loop(nx, body)
-
-    def feat_copy(buf, base, to, ss, rs, xx):
-        return remote(
-            buf.at[rows(base + xx * tl, tl)], to.at[rows(xx * tl, tl)],
-            ss.at[xx], rs.at[xx], sibling,
-        )
 
     def feat_own(left, right, out):
         def body(xx):
             cols = rows((xx * 2 + c) * tl, tl)
-            out[rows(xx * tl, tl), :] = tn(left[:, cols], right[...])
+            out[xx] = nn(left[...], right[:, cols])
 
         loop(nx, body)
 
@@ -329,10 +359,10 @@
     for j in range(wide):
         w_src[ITERS, j : j + 1, :] = line[:, j * 128 : (j + 1) * 128]
     dt = reduce_start(ITERS)
-    feat_out(s, pu, t_all, 0, ra, ra_s, ra_r)
+    feat_out(put, s, oa, ra, ra_s, ra_r)
     ds = reduce_middle(1, ds)
     dt = reduce_middle(ITERS, dt)
-    feat_own(s, pu, fa)
+    feat_own(put, s, fa)
     weights = 1.0 / (tokens * reduce_end(1, ds))
     lines = col_pass(weights)
     for j, line in enumerate(lines):
@@ -340,40 +370,86 @@
     row_pass(2)
     ds = reduce_start(2)
     for j, line in enumerate(lines):
-        ccol[j * 128 : (j + 1) * 128, :] = jnp.broadcast_to(line, (128, 128)).T
-
-    def scale_protos(j):
-        sl = rows(j * 128, 128)
-        anchor[sl, :] = (ccol[sl, 0:1] * pu[sl, :].astype(F32)).astype(BF)
-
-    loop(pl_rows // 128, scale_protos)
-    feat_out(e, anchor, t_all, nx * tl, rb, rb_s, rb_r)
+        sl = slice(j * 128, (j + 1) * 128)
+        anct[:, sl] = (put[:, sl].astype(F32) * line).astype(BF)
+    feat_out(anct, e, ob, rb, rb_s, rb_r)
     ds = reduce_middle(2, ds)
     w_out[wide : 2 * wide, :] = 1.0 / (student_temp * tokens * reduce_end(ITERS, dt))
-    feat_own(e, anchor, fb)
+    feat_own(anct, e, fb)
+    for j, line in enumerate(lines):
+        ccol[j * 128 : (j + 1) * 128, :] = jnp.broadcast_to(line, (128, 128)).T
 
     def column(j):
         return jnp.broadcast_to(w_out[pl.ds(j, 1), :], (128, 128)).T[:, 0:1]
 
     def student_weights(j):
         sl = rows(j * 128, 128)
-        st[sl, :] = (s_all[sl, :].astype(F32) * column(wide + j)).astype(BF)
+        t_all[sl, :] = (s_all[sl, :].astype(F32) * column(wide + j)).astype(BF)
 
     loop(wide, student_weights)
     tokens_drain(1)
     for xx in range(nx):
-        feat_copy(t_all, 0, ra, ra_s, ra_r, xx).wait()
-        feat_copy(t_all, nx * tl, rb, rb_s, rb_r, xx).wait()
+        feat_copy(oa, ra, ra_s, ra_r, xx).wait()
+        feat_copy(ob, rb, rb_s, rb_r, xx).wait()
     w_out[0:wide, :] = (1.0 / student_temp) / (tokens * reduce_end(2, ds))
 
+    def teacher_weights(j):
+        sl = rows(j * 128, 128)
+        s_all[sl, :] = (s_all[sl, :].astype(F32) * column(j)).astype(BF)
+
+    loop(wide, teacher_weights)
+
+    def chunk_part(block, q):
+        return gp_out.at[rows(block * pl_rows + q * CH, CH)]
+
+    def chunk_send(q, k):
+        to = (bat(1, 0), p) if k == 0 else (bat(nx - 1, 0), p)
+        part = chunk_part(b, q)
+        return remote(part, part, g_s.at[k, q], g_r.at[k, q], to)
+
+    def chunk_forward(q, k):
+        block = bat(nx - 1, 0) if k == 0 else bat(1, 0)
+        to = (bat(1, 0), p) if k == 0 else (bat(nx - 1, 0), p)
+        size = CH // 2
+        part = gp_out.at[rows(block * pl_rows + q * CH + k * size, size)]
+        return remote(part, part, f_s.at[k, q], f_r.at[k, q], to)
+
+    def chunk_sibling(q, k):
+        part = chunk_part(bat((0, nx - 1, 1, 2)[k], 0), q)
+        return remote(part, part, sib_s.at[k, q], sib_r.at[k, q], sibling)
+
+    def chunk_compute(q):
+        sl = rows(q * CH, CH)
+        back = nn(s[sl, :], t_all[...]) - ccol[sl, 0:1] * nn(e[sl, :], s_all[...])
+        unit, scale = unit_rows(sp[sl, :])
+        value = back_norm(back, unit, scale).astype(BF)
+        gp_out[rows(b * pl_rows + q * CH, CH), :] = value
+        chunk_send(q, 0).start()
+        chunk_send(q, 1).start()
+        chunk_sibling(q, 0).start()
+
+    def chunk_recv(q):
+        for k in range(2):
+            chunk_send(q, k).wait_recv()
+            chunk_forward(q, k).start()
+            chunk_sibling(q, 1 + k).start()
+
+    def chunk_last(q):
+        for k in range(2):
+            chunk_forward(q, k).wait_recv()
+        chunk_sibling(q, 3).start()
+
+    loop(2, chunk_compute)
+
     group = tl // 128
 
     def combine(i):
-        sl = rows(i * 128, 128)
-        j = ((i // group) * 2 + c) * group + lax.rem(i, group)
-        value = (fa[sl, :] + ra[sl, :].astype(F32)) * column(wide + j)
-        value = value - (fb[sl, :] + rb[sl, :].astype(F32)) * column(j)
-        cx[i // group, lax.rem(i, group)] = value.astype(BF).reshape(nz, piece, depth)
+        xx, g = i // group, lax.rem(i, group)
+        sl = rows(g * 128, 128)
+        j = (xx * 2 + c) * group + g
+        value = (fa[xx, :, sl] + ra[xx, :, sl].astype(F32)) * w_out[pl.ds(wide + j, 1), :]
+        value = value - (fb[xx, :, sl] + rb[xx, :, sl].astype(F32)) * w_out[pl.ds(j, 1), :]
+        cx[xx, g] = value.T.astype(BF).reshape(nz, piece, depth)
 
     loop(nx * group, combine)
     feat_d = []
@@ -456,66 +532,13 @@
             for j in range(1, nq)
         ]
 
-    def teacher_weights(j):
-        sl = rows(j * 128, 128)
-        s_all[sl, :] = (s_all[sl, :].astype(F32) * column(j)).astype(BF)
-
-    loop(wide, teacher_weights)
-
-    def chunk_part(block, q):
-        return gp_out.at[rows(block * pl_rows + q * CH, CH)]
-
-    def chunk_send(q, k):
-        to = (bat(1, 0), p) if k == 0 else (bat(nx - 1, 0), p)
-        part = chunk_part(b, q)
-        return remote(part, part, g_s.at[k, q], g_r.at[k, q], to)
-
-    def chunk_forward(q, k):
-        block = bat(nx - 1, 0) if k == 0 else bat(1, 0)
-        to = (bat(1, 0), p) if k == 0 else (bat(nx - 1, 0), p)
-        size = CH // 2
-        part = gp_out.at[rows(block * pl_rows + q * CH + k * size, size)]
-        return remote(part, part, f_s.at[k, q], f_r.at[k, q], to)
-
-    def chunk_sibling(q, k):
-        part = chunk_part(bat((0, nx - 1, 1, 2)[k], 0), q)
-        return remote(part, part, sib_s.at[k, q], sib_r.at[k, q], sibling)
-
-    def chunk_compute(q):
-        sl = rows(q * CH, CH)
-        back = nn(s[sl, :], st[...]) - ccol[sl, 0:1] * nn(e[sl, :], s_all[...])
-        unit, scale = unit_rows(sp[sl, :])
-        value = back_norm(back, unit, scale).astype(BF)
-        gp_out[rows(b * pl_rows + q * CH, CH), :] = value
-        chunk_send(q, 0).start()
-        chunk_send(q, 1).start()
-        chunk_sibling(q, 0).start()
-
-    def chunk_recv(q):
-        for k in range(2):
-            chunk_send(q, k).wait_recv()
-            chunk_forward(q, k).start()
-            chunk_sibling(q, 1 + k).start()
-
-    def chunk_last(q):
-        for k in range(2):
-            chunk_forward(q, k).wait_recv()
-        chunk_sibling(q, 3).start()
-
-    lag = 3
-    loop(lag, chunk_compute)
-
-    def chunk_both(q):
-        chunk_compute(q + lag)
-        chunk_recv(q)
-
-    loop(2, chunk_both)
+    loop(3, lambda q: chunk_compute(q + 2))
     second = feat_middle()
-    loop(chunks - lag - 2, lambda q: chunk_both(q + 2))
+    loop(chunks - 5, lambda q: chunk_compute(q + 5))
     third = feat_x(second)
-    chunk_recv(chunks - lag)
+    loop(chunks - 3, chunk_recv)
     final = feat_last(third)
-    loop(lag - 1, lambda q: chunk_recv(q + chunks - lag + 1))
+    loop(3, lambda q: chunk_recv(q + chunks - 3))
     loop(chunks, chunk_last)
 
     for d in pending + feat_d:
@@ -543,7 +566,6 @@
     piece = tl // nq
     vm = pltpu.VMEM
     dma = pltpu.SemaphoreType.DMA
-    half = tokens // 2
     hx, nz = nx // 2, NZ
     ny = nq // nz
     scratch = [
@@ -558,11 +580,14 @@
         vm((pl_rows, tokens), BF),
         vm((pl_rows, 128), F32),
         vm((8, tokens), F32),
-        vm((half, depth), F32),
-        vm((half, depth), F32),
-        vm((half, depth), BF),
-        vm((half, depth), BF),
-        vm((tokens, depth), BF),
+        vm((nx, depth, tl), F32),
+        vm((nx, depth, tl), F32),
+        vm((nx, depth, tl), BF),
+        vm((nx, depth, tl), BF),
+        vm((nx, depth, tl), BF),
+        vm((nx, depth, tl), BF),
+        vm((depth, pl_rows), BF),
+        vm((depth, pl_rows), BF),
         vm((pl_rows, 128), F32),
         vm((16, tokens), BF),
         vm((16, pl_rows), BF),
@@ -582,6 +607,7 @@
         vm((nx, piece, depth), BF),
         vm((nx - 1, piece, depth), BF),
         dma((4,)),
+        dma((2, nx, 2)), dma((2, nx, 2)), dma((2, nx, 2)), dma((2, nx, 2)),
         dma((2, nx)), dma((2, nx)), dma((2, nx)), dma((2, nx)),
         dma((2, nq - 1)), dma((2, nq - 1)),
         dma((ITERS + 1, nb - 1)), dma((ITERS + 1, nb - 1)),

time: 122 us -> 123 us (level); the launches traced: 122 us -> 121 us
  no operation moved by 1% of the time
where the time goes in v5:
time: 123 us; the launch traced here: 121 us
  Pallas kernels  117 us (95%)
  local copies, waits for them, and re-layouts  3.45 us (3%)
    pallas_call x1, Pallas kernels, on_device(): pl.pallas_call(functools.partial(kernel, nb, nq), out_shape=[pltpu.VMEM(s...  117 us
    unnamed x2, local copies, waits for them, and re-layouts  3.45 us

profile of v5, /device:TPU:0, one launch (start us, length us, event | category | flops | bytes accessed | tf_op | source)
XLA Modules:
  0.0 121.3 jit_solution(8217193541060481815)
XLA Ops:
  0.6 117.2 %prototype_head.1 = (bf16[8192,384]{1,0:T(8,128)(2,1)S(1)}, bf16[512,384]{1,0:T(8,128)(2,1)S(1)}) custom-call(bf16[512,384]{1,0:T(8,128)(2,1)} %sf_hbm.1, bf16[512,384]{1,0:T(8,128)(2,1)} %tf_hbm.1, bf16[8192,384]{1,0:T(8,128)(2,1)} %sp_hbm.1, bf16[8192,384]{1,0:T(8,128)(2,1)} %tp_hbm.1), custom_call_target="tpu_custom_call" | custom-call | tf_op jit(solution)/shard_map/prototype_head/pallas_call | solution.py:625
  117.8 2.7 %copy.8 = bf16[8192,384]{1,0:T(8,128)(2,1)} copy(bf16[8192,384]{1,0:T(8,128)(2,1)S(1)} %get-tuple-element.2) | data formatting | bytes 12582912
  120.5 0.7 copy.9

commit v6 on v5

--- a/solution.py
+++ b/solution.py
@@ -64,7 +64,7 @@
     sf, tf, t_all, s_all, sp, anchor, pu, e, s, cs, tot, fa, fb, ra, rb, oa, ob, put, anct, ccol,
     r16, c16, w_src, w_mid, w_g1, w_g2, w_out, cx, b1y, b1z, c2y, c2z, b2y, b2z, sumf, xs, xr,
     lsem, near_s, near_r, nfwd_s, nfwd_r, tok_s, tok_r, fwd_s, fwd_r, spr_s, spr_r,
-    a1_s, a1_r, a2_s, a2_r, g_s, g_r, f_s, f_r, sib_s, sib_r,
+    a1_s, a1_r, a2_s, a2_r, out_s, g_r, f_r, sib_r,
     ra_s, ra_r, rb_s, rb_r, y1_s, y1_r, z1_s, z1_r, y2_s, y2_r, z2_s, z2_r, xr_s, xr_r, gs_s, gs_r,
 ):
     nx = nb // 2
@@ -149,7 +149,11 @@
 
     def spread(f, j):
         part = feats[f].at[rows(bat(nx - far_dx, 0) * tl + p * piece, piece)]
-        return remote(part, part, spr_s.at[f, j - 1], spr_r.at[f, j - 1], peer(j))
+        return remote(part, part, spr_s.at[f], spr_r.at[f], peer(j))
+
+    def spread_all(f):
+        part = feats[f].at[0 : tl - piece]
+        return remote(part, part, spr_s.at[f], spr_r.at[f], sibling)
 
     def forward(f, dx):
         block = feats[f].at[rows(bat(nx - dx, 0) * tl, tl)]
@@ -170,15 +174,13 @@
             spread(f, j).start()
 
     def spread_end(f):
-        for j in range(1, nq):
-            spread(f, j).wait_recv()
+        spread_all(f).wait_recv()
         forward(f, far_dx).start()
 
-    def near_end(f):
-        for h in range(2):
-            for dx in near:
-                near_copy(f, dx, h).wait_recv()
-                near_forward(f, dx, h).start()
+    def near_part(f, h):
+        for dx in near:
+            near_copy(f, dx, h).wait_recv()
+            near_forward(f, dx, h).start()
 
     def tokens_drain(f):
         token_copy(f, far_dx).wait_send()
@@ -189,45 +191,40 @@
                 if f:
                     near_copy(f, dx, h).wait_send()
                 near_forward(f, dx, h).wait_send()
-        for j in range(1, nq):
-            spread(f, j).wait_send()
+        spread_all(f).wait_send()
 
     tokens_send(0)
     loads[2].wait()
     norm_into(anchor, anchor, 0, pl_rows)
 
-    def exp_plane(left, right, out, dx, factor, accumulate):
-        cols = rows(lax.rem(x + nx - dx, nx) * plane, plane)
+    def exp_block(left, right, out, block, width, factor, accumulate, first):
+        cols = pl.ds(pl.multiple_of(block * tl, width), width)
 
         def body(i):
             sl = rows(i * 256, 256)
             value = jnp.exp2(nt(left[sl, :], right[cols, :]) * factor)
             out[sl, cols] = value.astype(BF)
-            accumulate(value, sl, cols, dx)
+            accumulate(value, sl, cols, width, first)
 
         loop(pl_rows // 256, body)
 
-    def col_acc(value, sl, cols, dx):
+    def col_acc(value, sl, cols, width, first):
         acc = value[:, 0:128]
-        for q in range(1, plane // 128):
+        for q in range(1, width // 128):
             acc = acc + value[:, q * 128 : (q + 1) * 128]
-        if dx == 0:
+        if first:
             cs[sl, :] = acc
         else:
             cs[sl, :] += acc
 
-    def row_acc(value, sl, cols, dx):
-        tot[:, cols] += jnp.sum(value.reshape(32, 8, plane), axis=0)
-
-    def teacher_plane(dx):
-        if dx == far_dx:
-            forward(0, dx).wait_recv()
-        elif dx:
-            for h in range(2):
-                near_forward(0, dx, h).wait_recv()
-        else:
-            token_copy(0, 0).wait_recv()
-        exp_plane(anchor, t_all, e, dx, LOG2E / teacher_temp, col_acc)
+    def row_acc(value, sl, cols, width, first):
+        tot[:, cols] += jnp.sum(value.reshape(32, 8, width), axis=0)
+
+    def chip_block(dx):
+        return lax.rem(x + nx - dx, nx) * 2
+
+    def teacher_block(block, width, first=False):
+        exp_block(anchor, t_all, e, block, width, LOG2E / teacher_temp, col_acc, first)
 
     def student_plane(dx):
         if dx == far_dx:
@@ -237,11 +234,14 @@
                 near_forward(1, dx, h).wait_recv()
         else:
             token_copy(1, 0).wait_recv()
-        exp_plane(pu, s_all, s, dx, LOG2E / student_temp, row_acc)
+        exp_block(
+            pu, s_all, s, chip_block(dx), plane, LOG2E / student_temp, row_acc, False
+        )
 
     loads[1].wait()
     norm_into(sf, s_all, b * tl, tl)
-    teacher_plane(0)
+    token_copy(0, 0).wait_recv()
+    teacher_block(chip_block(0), plane, True)
     spread_start(0)
     loads[3].wait()
 
@@ -258,48 +258,51 @@
             near_copy(0, dx, h).wait_send()
     tokens_send(1)
     spread_end(0)
-    near_end(0)
-    teacher_plane(far_dx)
-    teacher_plane(near[0])
+    near_part(0, 0)
+    forward(0, far_dx).wait_recv()
+    teacher_block(chip_block(far_dx), plane)
+    near_part(0, 1)
+    for dx in near:
+        teacher_block(chip_block(dx) + c, tl)
     spread_start(1)
-    teacher_plane(near[1])
+    for dx in near:
+        for h in range(2):
+            near_forward(0, dx, h).wait_recv()
+        teacher_block(chip_block(dx) + 1 - c, tl)
     half = lax.broadcasted_iota(jnp.int32, (16, 128), 0) < 8
 
     def split_into(dst, j, row):
         high = row.astype(BF).astype(F32)
         dst[:, j * 128 : (j + 1) * 128] = jnp.where(half, high, row - high).astype(BF)
 
+    def first_step(n, j=1):
+        return remote(w_src.at[n], w_g1.at[n, j - 1], a1_s.at[n], a1_r.at[n],
+                      (lax.rem(b + j, nb), p))
+
+    def second_step(n, j=1):
+        return remote(w_mid.at[n], w_g2.at[n, j - 1], a2_s.at[n], a2_r.at[n], peer(j))
+
+    def first_all(n):
+        return remote(w_g1.at[n], w_g1.at[n], a1_s.at[n], a1_r.at[n], sibling)
+
+    def second_all(n):
+        return remote(w_g2.at[n], w_g2.at[n], a2_s.at[n], a2_r.at[n], sibling)
+
     def reduce_start(n):
-        ds = [
-            remote(w_src.at[n], w_g1.at[n, j - 1], a1_s.at[n, j - 1],
-                   a1_r.at[n, j - 1], (lax.rem(b + j, nb), p))
-            for j in range(1, nb)
-        ]
-        for d in ds:
-            d.start()
-        pending.extend(ds)
-        return ds
-
-    def reduce_middle(n, ds):
-        for d in ds:
-            d.wait_recv()
+        for j in range(1, nb):
+            first_step(n, j).start()
+
+    def reduce_middle(n):
+        first_all(n).wait_recv()
         value = w_src[n]
         for j in range(nb - 1):
             value = value + w_g1[n, j]
         w_mid[n] = value.astype(BF)
-        ds = [
-            remote(w_mid.at[n], w_g2.at[n, j - 1], a2_s.at[n, j - 1],
-                   a2_r.at[n, j - 1], peer(j))
-            for j in range(1, nq)
-        ]
-        for d in ds:
-            d.start()
-        pending.extend(ds)
-        return ds
-
-    def reduce_end(n, ds):
-        for d in ds:
-            d.wait_recv()
+        for j in range(1, nq):
+            second_step(n, j).start()
+
+    def reduce_end(n):
+        second_all(n).wait_recv()
         value = w_mid[n].astype(F32)
         for j in range(nq - 1):
             value = value + w_g2[n, j].astype(F32)
@@ -336,46 +339,46 @@
 
         loop(nx, body)
 
-    pending = []
     for j in range(pl_rows // 128):
         sums = jnp.sum(cs[j * 128 : (j + 1) * 128, :].T, axis=0, keepdims=True)
         split_into(c16, j, 1.0 / (protos * sums))
     row_pass(0)
-    ds = reduce_start(0)
+    reduce_start(0)
     student_plane(0)
     spread_end(1)
-    ds = reduce_middle(0, ds)
+    reduce_middle(0)
     student_plane(far_dx)
-    near_end(1)
+    near_part(1, 0)
+    near_part(1, 1)
     student_plane(near[0])
     student_plane(near[1])
     tokens_drain(0)
-    weights = 1.0 / (tokens * reduce_end(0, ds))
+    weights = 1.0 / (tokens * reduce_end(0))
     for j, line in enumerate(col_pass(weights)):
         split_into(c16, j, line)
     row_pass(1)
-    ds = reduce_start(1)
+    reduce_start(1)
+    feat_out(put, s, oa, ra, ra_s, ra_r)
+    reduce_middle(1)
     line = jnp.sum(tot[...], axis=0, keepdims=True)
     for j in range(wide):
         w_src[ITERS, j : j + 1, :] = line[:, j * 128 : (j + 1) * 128]
-    dt = reduce_start(ITERS)
-    feat_out(put, s, oa, ra, ra_s, ra_r)
-    ds = reduce_middle(1, ds)
-    dt = reduce_middle(ITERS, dt)
+    reduce_start(ITERS)
     feat_own(put, s, fa)
-    weights = 1.0 / (tokens * reduce_end(1, ds))
+    weights = 1.0 / (tokens * reduce_end(1))
     lines = col_pass(weights)
     for j, line in enumerate(lines):
         split_into(c16, j, line)
     row_pass(2)
-    ds = reduce_start(2)
+    reduce_start(2)
+    reduce_middle(ITERS)
     for j, line in enumerate(lines):
         sl = slice(j * 128, (j + 1) * 128)
         anct[:, sl] = (put[:, sl].astype(F32) * line).astype(BF)
     feat_out(anct, e, ob, rb, rb_s, rb_r)
-    ds = reduce_middle(2, ds)
-    w_out[wide : 2 * wide, :] = 1.0 / (student_temp * tokens * reduce_end(ITERS, dt))
+    reduce_middle(2)
     feat_own(anct, e, fb)
+    w_out[wide : 2 * wide, :] = 1.0 / (student_temp * tokens * reduce_end(ITERS))
     for j, line in enumerate(lines):
         ccol[j * 128 : (j + 1) * 128, :] = jnp.broadcast_to(line, (128, 128)).T
 
@@ -391,7 +394,7 @@
     for xx in range(nx):
         feat_copy(oa, ra, ra_s, ra_r, xx).wait()
         feat_copy(ob, rb, rb_s, rb_r, xx).wait()
-    w_out[0:wide, :] = (1.0 / student_temp) / (tokens * reduce_end(2, ds))
+    w_out[0:wide, :] = (1.0 / student_temp) / (tokens * reduce_end(2))
 
     def teacher_weights(j):
         sl = rows(j * 128, 128)
@@ -399,24 +402,28 @@
 
     loop(wide, teacher_weights)
 
-    def chunk_part(block, q):
-        return gp_out.at[rows(block * pl_rows + q * CH, CH)]
+    span = 2 * CH
+    groups = pl_rows // span
 
     def chunk_send(q, k):
         to = (bat(1, 0), p) if k == 0 else (bat(nx - 1, 0), p)
-        part = chunk_part(b, q)
-        return remote(part, part, g_s.at[k, q], g_r.at[k, q], to)
-
-    def chunk_forward(q, k):
+        part = gp_out.at[rows(b * pl_rows + q * CH, CH)]
+        return remote(part, part, out_s.at[0], g_r.at[k, q], to)
+
+    def group_forward(g, k):
         block = bat(nx - 1, 0) if k == 0 else bat(1, 0)
         to = (bat(1, 0), p) if k == 0 else (bat(nx - 1, 0), p)
-        size = CH // 2
-        part = gp_out.at[rows(block * pl_rows + q * CH + k * size, size)]
-        return remote(part, part, f_s.at[k, q], f_r.at[k, q], to)
-
-    def chunk_sibling(q, k):
-        part = chunk_part(bat((0, nx - 1, 1, 2)[k], 0), q)
-        return remote(part, part, sib_s.at[k, q], sib_r.at[k, q], sibling)
+        part = gp_out.at[rows(block * pl_rows + g * span + k * CH, CH)]
+        return remote(part, part, out_s.at[0], f_r.at[k, g], to)
+
+    def group_sibling(g, k):
+        block = bat((nx - 1, 1, 2)[k], 0)
+        part = gp_out.at[rows(block * pl_rows + g * span, span)]
+        return remote(part, part, out_s.at[0], sib_r.at[0], sibling)
+
+    def own_sibling():
+        part = gp_out.at[rows(b * pl_rows, pl_rows)]
+        return remote(part, part, out_s.at[0], sib_r.at[0], sibling)
 
     def chunk_compute(q):
         sl = rows(q * CH, CH)
@@ -426,18 +433,18 @@
         gp_out[rows(b * pl_rows + q * CH, CH), :] = value
         chunk_send(q, 0).start()
         chunk_send(q, 1).start()
-        chunk_sibling(q, 0).start()
-
-    def chunk_recv(q):
+
+    def group_recv(g):
         for k in range(2):
-            chunk_send(q, k).wait_recv()
-            chunk_forward(q, k).start()
-            chunk_sibling(q, 1 + k).start()
-
-    def chunk_last(q):
+            chunk_send(2 * g, k).wait_recv()
+            chunk_send(2 * g + 1, k).wait_recv()
+            group_forward(g, k).start()
+            group_sibling(g, k).start()
+
+    def group_last(g):
         for k in range(2):
-            chunk_forward(q, k).wait_recv()
-        chunk_sibling(q, 3).start()
+            group_forward(g, k).wait_recv()
+        group_sibling(g, 2).start()
 
     loop(2, chunk_compute)
 
@@ -452,13 +459,19 @@
         cx[xx, g] = value.T.astype(BF).reshape(nz, piece, depth)
 
     loop(nx * group, combine)
-    feat_d = []
-
     def feat_send(src, dst, ss, rs, to):
-        d = remote(src, dst, ss, rs, to)
-        d.start()
-        feat_d.append(d)
-        return d
+        remote(src, dst, ss, rs, to).start()
+
+    def whole(buf, ss, rs):
+        return remote(buf, buf, ss.at[0], rs.at[0], sibling)
+
+    first = [whole(b1y, y1_s, y1_r), whole(b1z, z1_s, z1_r)]
+    second = [whole(b2y, z2_s, z2_r), whole(b2z, y2_s, y2_r)]
+    third = whole(xr, xr_s, xr_r)
+    final = remote(
+        gs_out.at[0 : tl - piece], gs_out.at[0 : tl - piece],
+        gs_s.at[0], gs_r.at[0], sibling,
+    )
 
     def along_y(d):
         return lax.rem(y + d, ny)
@@ -466,15 +479,12 @@
     def along_z(d):
         return lax.rem(z + d, nz)
 
-    first = [
-        feat_send(cx.at[0:hx, along_y(d)], b1y.at[d - 1], y1_s.at[d - 1],
-                  y1_r.at[d - 1], (b, along_y(d) * nz + z))
-        for d in range(1, ny)
-    ] + [
-        feat_send(cx.at[hx:nx, :, along_z(d)], b1z.at[d - 1], z1_s.at[d - 1],
-                  z1_r.at[d - 1], (b, y * nz + along_z(d)))
-        for d in range(1, nz)
-    ]
+    for d in range(1, ny):
+        feat_send(cx.at[0:hx, along_y(d)], b1y.at[d - 1], y1_s.at[0],
+                  y1_r.at[0], (b, along_y(d) * nz + z))
+    for d in range(1, nz):
+        feat_send(cx.at[hx:nx, :, along_z(d)], b1z.at[d - 1], z1_s.at[0],
+                  z1_r.at[0], (b, y * nz + along_z(d)))
 
     def feat_middle():
         for d in first:
@@ -488,17 +498,14 @@
             for d in range(nz - 1):
                 value = value + b1z[d, h].astype(F32)
             c2z[h] = value.astype(BF)
-        return [
-            feat_send(c2y.at[:, along_z(d)], b2y.at[d - 1], z2_s.at[d - 1],
-                      z2_r.at[d - 1], (b, y * nz + along_z(d)))
-            for d in range(1, nz)
-        ] + [
-            feat_send(c2z.at[:, along_y(d)], b2z.at[d - 1], y2_s.at[d - 1],
-                      y2_r.at[d - 1], (b, along_y(d) * nz + z))
-            for d in range(1, ny)
-        ]
-
-    def feat_x(second):
+        for d in range(1, nz):
+            feat_send(c2y.at[:, along_z(d)], b2y.at[d - 1], z2_s.at[0],
+                      z2_r.at[0], (b, y * nz + along_z(d)))
+        for d in range(1, ny):
+            feat_send(c2z.at[:, along_y(d)], b2z.at[d - 1], y2_s.at[0],
+                      y2_r.at[0], (b, along_y(d) * nz + z))
+
+    def feat_x():
         for d in second:
             d.wait_recv()
         value = c2y[:, z].astype(F32)
@@ -511,15 +518,12 @@
             value = value + b2z[d].astype(F32)
         sumf[hx:nx] = value
         xs[hx:nx] = value.astype(BF)
-        return [
+        for dx in range(1, nx):
             feat_send(xs.at[lax.rem(x + dx, nx)], xr.at[dx - 1],
-                      xr_s.at[dx - 1], xr_r.at[dx - 1], (bat(dx, 0), p))
-            for dx in range(1, nx)
-        ]
-
-    def feat_last(third):
-        for d in third:
-            d.wait_recv()
+                      xr_s.at[0], xr_r.at[0], (bat(dx, 0), p))
+
+    def feat_last():
+        third.wait_recv()
         value = sumf[x]
         for dx in range(nx - 1):
             value = value + xr[dx].astype(F32)
@@ -527,33 +531,28 @@
         unit, scale = unit_rows(sf[own, :])
         gs_out[own, :] = back_norm(value, unit, scale).astype(BF)
         part = gs_out.at[own]
-        return [
-            feat_send(part, part, gs_s.at[j - 1], gs_r.at[j - 1], peer(j))
-            for j in range(1, nq)
-        ]
-
-    loop(3, lambda q: chunk_compute(q + 2))
-    second = feat_middle()
-    loop(chunks - 5, lambda q: chunk_compute(q + 5))
-    third = feat_x(second)
-    loop(chunks - 3, chunk_recv)
-    final = feat_last(third)
-    loop(3, lambda q: chunk_recv(q + chunks - 3))
-    loop(chunks, chunk_last)
-
-    for d in pending + feat_d:
+        for j in range(1, nq):
+            feat_send(part, part, gs_s.at[0], gs_r.at[0], peer(j))
+
+    loop(chunks - 2, lambda q: chunk_compute(q + 2))
+    own_sibling().start()
+    feat_middle()
+    loop(groups, group_recv)
+    feat_x()
+    loop(groups // 2, group_last)
+    feat_last()
+    loop(groups // 2, lambda g: group_last(g + groups // 2))
+
+    for n in range(ITERS + 1):
+        first_all(n).wait_send()
+        second_all(n).wait_send()
+    for d in first + second + [third, final]:
         d.wait_send()
-
-    def drain(q):
-        for k in range(2):
-            chunk_send(q, k).wait_send()
-            chunk_forward(q, k).wait_send()
-        for k in range(4):
-            chunk_sibling(q, k).wait()
-
-    loop(chunks, drain)
-    for d in final:
-        d.wait_recv()
+    sent = gp_out.at[0 : pl_rows * (nx + 3)]
+    remote(sent, sent, out_s.at[0], sib_r.at[0], sibling).wait_send()
+    held = gp_out.at[0 : pl_rows * nx]
+    remote(held, held, out_s.at[0], sib_r.at[0], sibling).wait_recv()
+    final.wait_recv()
 
 
 def on_device(nb, nq, student_feats, teacher_feats, student_protos, teacher_protos):
@@ -609,16 +608,13 @@
         dma((4,)),
         dma((2, nx, 2)), dma((2, nx, 2)), dma((2, nx, 2)), dma((2, nx, 2)),
         dma((2, nx)), dma((2, nx)), dma((2, nx)), dma((2, nx)),
-        dma((2, nq - 1)), dma((2, nq - 1)),
-        dma((ITERS + 1, nb - 1)), dma((ITERS + 1, nb - 1)),
-        dma((ITERS + 1, nq - 1)), dma((ITERS + 1, nq - 1)),
-        dma((2, chunks)), dma((2, chunks)), dma((2, chunks)), dma((2, chunks)),
-        dma((4, chunks)), dma((4, chunks)),
+        dma((2,)), dma((2,)),
+        dma((ITERS + 1,)), dma((ITERS + 1,)),
+        dma((ITERS + 1,)), dma((ITERS + 1,)),
+        dma((1,)), dma((2, chunks)), dma((2, chunks // 2)), dma((1,)),
         dma((nx,)), dma((nx,)), dma((nx,)), dma((nx,)),
-        dma((ny - 1,)), dma((ny - 1,)), dma((nz - 1,)), dma((nz - 1,)),
-        dma((ny - 1,)), dma((ny - 1,)), dma((nz - 1,)), dma((nz - 1,)),
-        dma((nx - 1,)), dma((nx - 1,)),
-        dma((nq - 1,)), dma((nq - 1,)),
+        dma((1,)), dma((1,)), dma((1,)), dma((1,)), dma((1,)), dma((1,)),
+        dma((1,)), dma((1,)), dma((1,)), dma((1,)), dma((1,)), dma((1,)),
     ]
     in_vmem = pl.BlockSpec(memory_space=pltpu.VMEM)
     anywhere = pl.BlockSpec(memory_space=pl.ANY)

time: 123 us -> 120 us (0.976); the launches traced: 121 us -> 120 us
  no operation moved by 1% of the time
where the time goes in v6:
time: 120 us
  Pallas kernels  116 us (97%)
  local copies, waits for them, and re-layouts  3.45 us (3%)
    pallas_call x1, Pallas kernels, on_device(): pl.pallas_call(functools.partial(kernel, nb, nq), out_shape=[pltpu.VMEM(s...  116 us
    unnamed x2, local copies, waits for them, and re-layouts  3.45 us

profile of v6, /device:TPU:0, one launch (start us, length us, event | category | flops | bytes accessed | tf_op | source)
XLA Modules:
  0.0 120.3 jit_solution(7133694816850120336)
XLA Ops:
  0.6 116.2 %prototype_head.1 = (bf16[8192,384]{1,0:T(8,128)(2,1)S(1)}, bf16[512,384]{1,0:T(8,128)(2,1)S(1)}) custom-call(bf16[512,384]{1,0:T(8,128)(2,1)} %sf_hbm.1, bf16[512,384]{1,0:T(8,128)(2,1)} %tf_hbm.1, bf16[8192,384]{1,0:T(8,128)(2,1)} %sp_hbm.1, bf16[8192,384]{1,0:T(8,128)(2,1)} %tp_hbm.1), custom_call_target="tpu_custom_call" | custom-call | tf_op jit(solution)/shard_map/prototype_head/pallas_call | solution.py:621
  116.8 2.7 %copy.8 = bf16[8192,384]{1,0:T(8,128)(2,1)} copy(bf16[8192,384]{1,0:T(8,128)(2,1)S(1)} %get-tuple-element.2) | data formatting | bytes 12582912
  119.5 0.7 copy.9

commit v7 on v6

--- a/solution.py
+++ b/solution.py
@@ -396,58 +396,6 @@
         feat_copy(ob, rb, rb_s, rb_r, xx).wait()
     w_out[0:wide, :] = (1.0 / student_temp) / (tokens * reduce_end(2))
 
-    def teacher_weights(j):
-        sl = rows(j * 128, 128)
-        s_all[sl, :] = (s_all[sl, :].astype(F32) * column(j)).astype(BF)
-
-    loop(wide, teacher_weights)
-
-    span = 2 * CH
-    groups = pl_rows // span
-
-    def chunk_send(q, k):
-        to = (bat(1, 0), p) if k == 0 else (bat(nx - 1, 0), p)
-        part = gp_out.at[rows(b * pl_rows + q * CH, CH)]
-        return remote(part, part, out_s.at[0], g_r.at[k, q], to)
-
-    def group_forward(g, k):
-        block = bat(nx - 1, 0) if k == 0 else bat(1, 0)
-        to = (bat(1, 0), p) if k == 0 else (bat(nx - 1, 0), p)
-        part = gp_out.at[rows(block * pl_rows + g * span + k * CH, CH)]
-        return remote(part, part, out_s.at[0], f_r.at[k, g], to)
-
-    def group_sibling(g, k):
-        block = bat((nx - 1, 1, 2)[k], 0)
-        part = gp_out.at[rows(block * pl_rows + g * span, span)]
-        return remote(part, part, out_s.at[0], sib_r.at[0], sibling)
-
-    def own_sibling():
-        part = gp_out.at[rows(b * pl_rows, pl_rows)]
-        return remote(part, part, out_s.at[0], sib_r.at[0], sibling)
-
-    def chunk_compute(q):
-        sl = rows(q * CH, CH)
-        back = nn(s[sl, :], t_all[...]) - ccol[sl, 0:1] * nn(e[sl, :], s_all[...])
-        unit, scale = unit_rows(sp[sl, :])
-        value = back_norm(back, unit, scale).astype(BF)
-        gp_out[rows(b * pl_rows + q * CH, CH), :] = value
-        chunk_send(q, 0).start()
-        chunk_send(q, 1).start()
-
-    def group_recv(g):
-        for k in range(2):
-            chunk_send(2 * g, k).wait_recv()
-            chunk_send(2 * g + 1, k).wait_recv()
-            group_forward(g, k).start()
-            group_sibling(g, k).start()
-
-    def group_last(g):
-        for k in range(2):
-            group_forward(g, k).wait_recv()
-        group_sibling(g, 2).start()
-
-    loop(2, chunk_compute)
-
     group = tl // 128
 
     def combine(i):
@@ -534,14 +482,65 @@
         for j in range(1, nq):
             feat_send(part, part, gs_s.at[0], gs_r.at[0], peer(j))
 
-    loop(chunks - 2, lambda q: chunk_compute(q + 2))
+    def teacher_weights(j):
+        sl = rows(j * 128, 128)
+        s_all[sl, :] = (s_all[sl, :].astype(F32) * column(j)).astype(BF)
+
+    loop(wide, teacher_weights)
+
+    span = 2 * CH
+    groups = pl_rows // span
+
+    def chunk_send(q, k):
+        to = (bat(1, 0), p) if k == 0 else (bat(nx - 1, 0), p)
+        part = gp_out.at[rows(b * pl_rows + q * CH, CH)]
+        return remote(part, part, out_s.at[0], g_r.at[k, q], to)
+
+    def group_forward(g, k):
+        block = bat(nx - 1, 0) if k == 0 else bat(1, 0)
+        to = (bat(1, 0), p) if k == 0 else (bat(nx - 1, 0), p)
+        part = gp_out.at[rows(block * pl_rows + g * span + k * CH, CH)]
+        return remote(part, part, out_s.at[0], f_r.at[k, g], to)
+
+    def group_sibling(g, k):
+        block = bat((nx - 1, 1, 2)[k], 0)
+        part = gp_out.at[rows(block * pl_rows + g * span, span)]
+        return remote(part, part, out_s.at[0], sib_r.at[0], sibling)
+
+    def own_sibling():
+        part = gp_out.at[rows(b * pl_rows, pl_rows)]
+        return remote(part, part, out_s.at[0], sib_r.at[0], sibling)
+
+    def chunk_compute(q):
+        sl = rows(q * CH, CH)
+        back = nn(s[sl, :], t_all[...]) - ccol[sl, 0:1] * nn(e[sl, :], s_all[...])
+        unit, scale = unit_rows(sp[sl, :])
+        value = back_norm(back, unit, scale).astype(BF)
+        gp_out[rows(b * pl_rows + q * CH, CH), :] = value
+        chunk_send(q, 0).start()
+        chunk_send(q, 1).start()
+
+    def group_recv(g):
+        for k in range(2):
+            chunk_send(2 * g, k).wait_recv()
+            chunk_send(2 * g + 1, k).wait_recv()
+            group_forward(g, k).start()
+            group_sibling(g, k).start()
+
+    def group_last(g):
+        for k in range(2):
+            group_forward(g, k).wait_recv()
+        group_sibling(g, 2).start()
+
+    loop(5, chunk_compute)
+    feat_middle()
+    loop(chunks - 5, lambda q: chunk_compute(q + 5))
     own_sibling().start()
-    feat_middle()
-    loop(groups, group_recv)
     feat_x()
-    loop(groups // 2, group_last)
+    loop(groups - 1, group_recv)
     feat_last()
-    loop(groups // 2, lambda g: group_last(g + groups // 2))
+    group_recv(groups - 1)
+    loop(groups, group_last)
 
     for n in range(ITERS + 1):
         first_all(n).wait_send()

time: 120 us -> 117 us (0.975); the launches traced: 120 us -> 116 us
  Pallas kernels: 116 us -> 111 us
    pallas_call x1, Pallas kernels: 116 us -> 111 us  [on_device(): pl.pallas_call(functools.partial(kernel, nb, nq), out_shape=[pltpu.VMEM(s...]
where the time goes in v7:
time: 117 us; the launch traced here: 116 us
  Pallas kernels  111 us (95%)
  local copies, waits for them, and re-layouts  3.45 us (3%)
    pallas_call x1, Pallas kernels, on_device(): pl.pallas_call(functools.partial(kernel, nb, nq), out_shape=[pltpu.VMEM(s...  111 us
    unnamed x2, local copies, waits for them, and re-layouts  3.45 us

profile of v7, /device:TPU:0, one launch (start us, length us, event | category | flops | bytes accessed | tf_op | source)
XLA Modules:
  0.0 115.6 jit_solution(14632161063498666255)
XLA Ops:
  0.6 111.5 %prototype_head.1 = (bf16[8192,384]{1,0:T(8,128)(2,1)S(1)}, bf16[512,384]{1,0:T(8,128)(2,1)S(1)}) custom-call(bf16[512,384]{1,0:T(8,128)(2,1)} %sf_hbm.1, bf16[512,384]{1,0:T(8,128)(2,1)} %tf_hbm.1, bf16[8192,384]{1,0:T(8,128)(2,1)} %sp_hbm.1, bf16[8192,384]{1,0:T(8,128)(2,1)} %tp_hbm.1), custom_call_target="tpu_custom_call" | custom-call | tf_op jit(solution)/shard_map/prototype_head/pallas_call | solution.py:620
  112.1 2.7 %copy.8 = bf16[8192,384]{1,0:T(8,128)(2,1)} copy(bf16[8192,384]{1,0:T(8,128)(2,1)S(1)} %get-tuple-element.2) | data formatting | bytes 12582912
  114.8 0.7 copy.9

commit v8 on v7

--- a/solution.py
+++ b/solution.py
@@ -62,7 +62,7 @@
     sf_hbm, tf_hbm, sp_hbm, tp_hbm,
     gp_out, gs_out,
     sf, tf, t_all, s_all, sp, anchor, pu, e, s, cs, tot, fa, fb, ra, rb, oa, ob, put, anct, ccol,
-    r16, c16, w_src, w_mid, w_g1, w_g2, w_out, cx, b1y, b1z, c2y, c2z, b2y, b2z, sumf, xs, xr,
+    r16, c16, w_src, w_mid, w_g1, w_g2, w_row, delta, cx, b1y, b1z, c2y, c2z, b2y, b2z, sumf, xs, xr,
     lsem, near_s, near_r, nfwd_s, nfwd_r, tok_s, tok_r, fwd_s, fwd_r, spr_s, spr_r,
     a1_s, a1_r, a2_s, a2_r, out_s, g_r, f_r, sib_r,
     ra_s, ra_r, rb_s, rb_r, y1_s, y1_r, z1_s, z1_r, y2_s, y2_r, z2_s, z2_r, xr_s, xr_r, gs_s, gs_r,
@@ -307,6 +307,12 @@
         for j in range(nq - 1):
             value = value + w_g2[n, j].astype(F32)
         return value
+
+    def spread_rows(k, weights):
+        for j in range(wide):
+            w_row[k, :, j * 128 : (j + 1) * 128] = jnp.broadcast_to(
+                weights[j : j + 1, :], (8, 128)
+            )
 
     def row_pass(n):
         out = nn(c16[...], e[...])
@@ -378,32 +384,25 @@
     feat_out(anct, e, ob, rb, rb_s, rb_r)
     reduce_middle(2)
     feat_own(anct, e, fb)
-    w_out[wide : 2 * wide, :] = 1.0 / (student_temp * tokens * reduce_end(ITERS))
+    spread_rows(1, 1.0 / (student_temp * tokens * reduce_end(ITERS)))
     for j, line in enumerate(lines):
         ccol[j * 128 : (j + 1) * 128, :] = jnp.broadcast_to(line, (128, 128)).T
 
-    def column(j):
-        return jnp.broadcast_to(w_out[pl.ds(j, 1), :], (128, 128)).T[:, 0:1]
-
-    def student_weights(j):
-        sl = rows(j * 128, 128)
-        t_all[sl, :] = (s_all[sl, :].astype(F32) * column(wide + j)).astype(BF)
-
-    loop(wide, student_weights)
+
     tokens_drain(1)
     for xx in range(nx):
         feat_copy(oa, ra, ra_s, ra_r, xx).wait()
         feat_copy(ob, rb, rb_s, rb_r, xx).wait()
-    w_out[0:wide, :] = (1.0 / student_temp) / (tokens * reduce_end(2))
+    spread_rows(0, (1.0 / student_temp) / (tokens * reduce_end(2)))
 
     group = tl // 128
 
     def combine(i):
         xx, g = i // group, lax.rem(i, group)
         sl = rows(g * 128, 128)
-        j = (xx * 2 + c) * group + g
-        value = (fa[xx, :, sl] + ra[xx, :, sl].astype(F32)) * w_out[pl.ds(wide + j, 1), :]
-        value = value - (fb[xx, :, sl] + rb[xx, :, sl].astype(F32)) * w_out[pl.ds(j, 1), :]
+        at = rows(((xx * 2 + c) * group + g) * 128, 128)
+        value = (fa[xx, :, sl] + ra[xx, :, sl].astype(F32)) * w_row[1, 0:1, at]
+        value = value - (fb[xx, :, sl] + rb[xx, :, sl].astype(F32)) * w_row[0, 0:1, at]
         cx[xx, g] = value.T.astype(BF).reshape(nz, piece, depth)
 
     loop(nx * group, combine)
@@ -482,12 +481,6 @@
         for j in range(1, nq):
             feat_send(part, part, gs_s.at[0], gs_r.at[0], peer(j))
 
-    def teacher_weights(j):
-        sl = rows(j * 128, 128)
-        s_all[sl, :] = (s_all[sl, :].astype(F32) * column(j)).astype(BF)
-
-    loop(wide, teacher_weights)
-
     span = 2 * CH
     groups = pl_rows // span
 
@@ -513,7 +506,13 @@
 
     def chunk_compute(q):
         sl = rows(q * CH, CH)
-        back = nn(s[sl, :], t_all[...]) - ccol[sl, 0:1] * nn(e[sl, :], s_all[...])
+        weight = ccol[sl, 0:1]
+        for j in range(tokens // 512):
+            js = slice(j * 512, (j + 1) * 512)
+            value = s[sl, js].astype(F32) * w_row[1, 0:1, js]
+            value = value - e[sl, js].astype(F32) * (w_row[0, 0:1, js] * weight)
+            delta[:, js] = value.astype(BF)
+        back = nn(delta[...], s_all[...])
         unit, scale = unit_rows(sp[sl, :])
         value = back_norm(back, unit, scale).astype(BF)
         gp_out[rows(b * pl_rows + q * CH, CH), :] = value
@@ -532,10 +531,9 @@
             group_forward(g, k).wait_recv()
         group_sibling(g, 2).start()
 
-    loop(5, chunk_compute)
+    loop(chunks, chunk_compute)
+    own_sibling().start()
     feat_middle()
-    loop(chunks - 5, lambda q: chunk_compute(q + 5))
-    own_sibling().start()
     feat_x()
     loop(groups - 1, group_recv)
     feat_last()
@@ -593,7 +591,8 @@
         vm((ITERS + 1, wide, 128), BF),
         vm((ITERS + 1, nb - 1, wide, 128), F32),
         vm((ITERS + 1, nq - 1, wide, 128), BF),
-        vm((2 * wide, 128), F32),
+        vm((2, 8, tokens), F32),
+        vm((CH, tokens), BF),
         vm((nx, ny, nz, piece, depth), BF),
         vm((ny - 1, hx, nz, piece, depth), BF),
         vm((nz - 1, hx, ny, piece, depth), BF),

time: 117 us -> 107 us (0.915)
  Pallas kernels: 111 us -> 101 us
    pallas_call x1, Pallas kernels: 111 us -> 101 us  [on_device(): pl.pallas_call(functools.partial(kernel, nb, nq), out_shape=[pltpu.VMEM(s...]
where the time goes in v8:
time: 107 us; the launch traced here: 105 us
  Pallas kernels  101 us (94%)
  local copies, waits for them, and re-layouts  3.45 us (3%)
    pallas_call x1, Pallas kernels, on_device(): pl.pallas_call(functools.partial(kernel, nb, nq), out_shape=[pltpu.VMEM(s...  101 us
    unnamed x2, local copies, waits for them, and re-layouts  3.45 us

profile of v8, /device:TPU:0, one launch (start us, length us, event | category | flops | bytes accessed | tf_op | source)
XLA Modules:
  0.0 105.3 jit_solution(14520348524677255582)
XLA Ops:
  0.6 101.2 %prototype_head.1 = (bf16[8192,384]{1,0:T(8,128)(2,1)S(1)}, bf16[512,384]{1,0:T(8,128)(2,1)S(1)}) custom-call(bf16[512,384]{1,0:T(8,128)(2,1)} %sf_hbm.1, bf16[512,384]{1,0:T(8,128)(2,1)} %tf_hbm.1, bf16[8192,384]{1,0:T(8,128)(2,1)} %sp_hbm.1, bf16[8192,384]{1,0:T(8,128)(2,1)} %tp_hbm.1), custom_call_target="tpu_custom_call" | custom-call | tf_op jit(solution)/shard_map/prototype_head/pallas_call | solution.py:619
  101.9 2.7 %copy.8 = bf16[8192,384]{1,0:T(8,128)(2,1)} copy(bf16[8192,384]{1,0:T(8,128)(2,1)S(1)} %get-tuple-element.2) | data formatting | bytes 12582912
  104.6 0.7 copy.9

commit v9 on v8

--- a/solution.py
+++ b/solution.py
@@ -87,8 +87,17 @@
     def bat(dx, dc):
         return lax.rem(x + dx, nx) * 2 + lax.rem(c + dc, 2)
 
-    def peer(j):
-        return (b, lax.rem(p + j, nq))
+    def hops(d, n):
+        return min(d, n - d)
+
+    ys = [lax.rem(y + d, ny) for d in range(ny)]
+    zs = [lax.rem(z + d, nz) for d in range(nz)]
+    steps = [(dy, dz) for dy in range(ny) for dz in range(nz) if dy or dz]
+    steps.sort(key=lambda d: -hops(d[0], ny) - hops(d[1], nz))
+    proto_peers = [(dy * nz + dz - 1, (b, ys[dy] * nz + zs[dz])) for dy, dz in steps]
+    steps = [(dx, dc) for dx in range(nx) for dc in range(2) if dx or dc]
+    steps.sort(key=lambda d: -2 * hops(d[0], nx) - d[1])
+    batch_peers = [(dx * 2 + dc - 1, (bat(dx, dc), p)) for dx, dc in steps]
 
     def remote(src, dst, ss, rs, to):
         return pltpu.make_async_remote_copy(
@@ -98,12 +107,8 @@
     sibling = (bat(0, 1), p)
 
     barrier = pltpu.get_barrier_semaphore()
-    for j in range(1, nb):
-        pl.semaphore_signal(
-            barrier, inc=1, device_id=(lax.rem(b + j, nb), p), device_id_type=MESH
-        )
-    for j in range(1, nq):
-        pl.semaphore_signal(barrier, inc=1, device_id=peer(j), device_id_type=MESH)
+    for _, to in proto_peers + batch_peers:
+        pl.semaphore_signal(barrier, inc=1, device_id=to, device_id_type=MESH)
     mine = rows(b * pl_rows, pl_rows)
     loads = [
         pltpu.make_async_copy(tf_hbm, tf, lsem.at[0]),
@@ -147,9 +152,9 @@
         to = sibling if dx == 0 else (bat(dx, 0), p)
         return remote(part, part, tok_s.at[f, dx], tok_r.at[f, dx], to)
 
-    def spread(f, j):
+    def spread(f, to):
         part = feats[f].at[rows(bat(nx - far_dx, 0) * tl + p * piece, piece)]
-        return remote(part, part, spr_s.at[f], spr_r.at[f], peer(j))
+        return remote(part, part, spr_s.at[f], spr_r.at[f], to)
 
     def spread_all(f):
         part = feats[f].at[0 : tl - piece]
@@ -170,8 +175,8 @@
 
     def spread_start(f):
         token_copy(f, far_dx).wait_recv()
-        for j in range(1, nq):
-            spread(f, j).start()
+        for _, to in proto_peers:
+            spread(f, to).start()
 
     def spread_end(f):
         spread_all(f).wait_recv()
@@ -264,7 +269,6 @@
     near_part(0, 1)
     for dx in near:
         teacher_block(chip_block(dx) + c, tl)
-    spread_start(1)
     for dx in near:
         for h in range(2):
             near_forward(0, dx, h).wait_recv()
@@ -275,12 +279,11 @@
         high = row.astype(BF).astype(F32)
         dst[:, j * 128 : (j + 1) * 128] = jnp.where(half, high, row - high).astype(BF)
 
-    def first_step(n, j=1):
-        return remote(w_src.at[n], w_g1.at[n, j - 1], a1_s.at[n], a1_r.at[n],
-                      (lax.rem(b + j, nb), p))
-
-    def second_step(n, j=1):
-        return remote(w_mid.at[n], w_g2.at[n, j - 1], a2_s.at[n], a2_r.at[n], peer(j))
+    def first_step(n, slot, to):
+        return remote(w_src.at[n], w_g1.at[n, slot], a1_s.at[n], a1_r.at[n], to)
+
+    def second_step(n, slot, to):
+        return remote(w_mid.at[n], w_g2.at[n, slot], a2_s.at[n], a2_r.at[n], to)
 
     def first_all(n):
         return remote(w_g1.at[n], w_g1.at[n], a1_s.at[n], a1_r.at[n], sibling)
@@ -289,8 +292,8 @@
         return remote(w_g2.at[n], w_g2.at[n], a2_s.at[n], a2_r.at[n], sibling)
 
     def reduce_start(n):
-        for j in range(1, nb):
-            first_step(n, j).start()
+        for slot, to in batch_peers:
+            first_step(n, slot, to).start()
 
     def reduce_middle(n):
         first_all(n).wait_recv()
@@ -298,8 +301,8 @@
         for j in range(nb - 1):
             value = value + w_g1[n, j]
         w_mid[n] = value.astype(BF)
-        for j in range(1, nq):
-            second_step(n, j).start()
+        for slot, to in proto_peers:
+            second_step(n, slot, to).start()
 
     def reduce_end(n):
         second_all(n).wait_recv()
@@ -350,14 +353,15 @@
         split_into(c16, j, 1.0 / (protos * sums))
     row_pass(0)
     reduce_start(0)
+    spread_start(1)
     student_plane(0)
-    spread_end(1)
     reduce_middle(0)
-    student_plane(far_dx)
     near_part(1, 0)
     near_part(1, 1)
+    spread_end(1)
     student_plane(near[0])
     student_plane(near[1])
+    student_plane(far_dx)
     tokens_drain(0)
     weights = 1.0 / (tokens * reduce_end(0))
     for j, line in enumerate(col_pass(weights)):
@@ -478,8 +482,8 @@
         unit, scale = unit_rows(sf[own, :])
         gs_out[own, :] = back_norm(value, unit, scale).astype(BF)
         part = gs_out.at[own]
-        for j in range(1, nq):
-            feat_send(part, part, gs_s.at[0], gs_r.at[0], peer(j))
+        for _, to in proto_peers:
+            feat_send(part, part, gs_s.at[0], gs_r.at[0], to)
 
     span = 2 * CH
     groups = pl_rows // span

time: 107 us -> 105 us (0.981)
  Pallas kernels: 101 us -> 99.6 us
    pallas_call x1, Pallas kernels: 101 us -> 99.6 us  [on_device(): pl.pallas_call(functools.partial(kernel, nb, nq), out_shape=[pltpu.VMEM(s...]
where the time goes in v9:
time: 105 us; the launch traced here: 104 us
  Pallas kernels  99.6 us (95%)
  local copies, waits for them, and re-layouts  3.45 us (3%)
    pallas_call x1, Pallas kernels, on_device(): pl.pallas_call(functools.partial(kernel, nb, nq), out_shape=[pltpu.VMEM(s...  99.6 us
    unnamed x2, local copies, waits for them, and re-layouts  3.45 us

profile of v9, /device:TPU:0, one launch (start us, length us, event | category | flops | bytes accessed | tf_op | source)
XLA Modules:
  0.0 103.7 jit_solution(10847998202554494510)
XLA Ops:
  0.6 99.6 %prototype_head.1 = (bf16[8192,384]{1,0:T(8,128)(2,1)S(1)}, bf16[512,384]{1,0:T(8,128)(2,1)S(1)}) custom-call(bf16[512,384]{1,0:T(8,128)(2,1)} %sf_hbm.1, bf16[512,384]{1,0:T(8,128)(2,1)} %tf_hbm.1, bf16[8192,384]{1,0:T(8,128)(2,1)} %sp_hbm.1, bf16[8192,384]{1,0:T(8,128)(2,1)} %tp_hbm.1), custom_call_target="tpu_custom_call" | custom-call | tf_op jit(solution)/shard_map/prototype_head/pallas_call | solution.py:623
  100.2 2.7 %copy.8 = bf16[8192,384]{1,0:T(8,128)(2,1)} copy(bf16[8192,384]{1,0:T(8,128)(2,1)S(1)} %get-tuple-element.2) | data formatting | bytes 12582912
  102.9 0.7 copy.9

commit v10 on v9

--- a/solution.py
+++ b/solution.py
@@ -245,9 +245,9 @@
 
     loads[1].wait()
     norm_into(sf, s_all, b * tl, tl)
+    spread_start(0)
     token_copy(0, 0).wait_recv()
     teacher_block(chip_block(0), plane, True)
-    spread_start(0)
     loads[3].wait()
 
     def norm_protos(i):
@@ -256,6 +256,7 @@
         pu[sl, :] = unit.astype(BF)
         put[:, sl] = unit.T.astype(BF)
 
+    near_part(0, 0)
     loop(pl_rows // 128, norm_protos)
     tot[...] = jnp.zeros_like(tot)
     for h in range(2):
@@ -263,12 +264,11 @@
             near_copy(0, dx, h).wait_send()
     tokens_send(1)
     spread_end(0)
-    near_part(0, 0)
-    forward(0, far_dx).wait_recv()
-    teacher_block(chip_block(far_dx), plane)
     near_part(0, 1)
     for dx in near:
         teacher_block(chip_block(dx) + c, tl)
+    forward(0, far_dx).wait_recv()
+    teacher_block(chip_block(far_dx), plane)
     for dx in near:
         for h in range(2):
             near_forward(0, dx, h).wait_recv()
@@ -399,6 +399,58 @@
         feat_copy(ob, rb, rb_s, rb_r, xx).wait()
     spread_rows(0, (1.0 / student_temp) / (tokens * reduce_end(2)))
 
+    span = 2 * CH
+    groups = pl_rows // span
+
+    def chunk_send(q, k):
+        to = (bat(1, 0), p) if k == 0 else (bat(nx - 1, 0), p)
+        part = gp_out.at[rows(b * pl_rows + q * CH, CH)]
+        return remote(part, part, out_s.at[0], g_r.at[k, q], to)
+
+    def group_forward(g, k):
+        block = bat(nx - 1, 0) if k == 0 else bat(1, 0)
+        to = (bat(1, 0), p) if k == 0 else (bat(nx - 1, 0), p)
+        part = gp_out.at[rows(block * pl_rows + g * span + k * CH, CH)]
+        return remote(part, part, out_s.at[0], f_r.at[k, g], to)
+
+    def group_sibling(g, k):
+        block = bat((nx - 1, 1, 2)[k], 0)
+        part = gp_out.at[rows(block * pl_rows + g * span, span)]
+        return remote(part, part, out_s.at[0], sib_r.at[0], sibling)
+
+    def own_sibling():
+        part = gp_out.at[rows(b * pl_rows, pl_rows)]
+        return remote(part, part, out_s.at[0], sib_r.at[0], sibling)
+
+    def chunk_compute(q):
+        sl = rows(q * CH, CH)
+        weight = ccol[sl, 0:1]
+        for j in range(tokens // 512):
+            js = slice(j * 512, (j + 1) * 512)
+            value = s[sl, js].astype(F32) * w_row[1, 0:1, js]
+            value = value - e[sl, js].astype(F32) * (w_row[0, 0:1, js] * weight)
+            delta[:, js] = value.astype(BF)
+        back = nn(delta[...], s_all[...])
+        unit, scale = unit_rows(sp[sl, :])
+        value = back_norm(back, unit, scale).astype(BF)
+        gp_out[rows(b * pl_rows + q * CH, CH), :] = value
+        chunk_send(q, 0).start()
+        chunk_send(q, 1).start()
+
+    def group_recv(g):
+        for k in range(2):
+            chunk_send(2 * g, k).wait_recv()
+            chunk_send(2 * g + 1, k).wait_recv()
+            group_forward(g, k).start()
+            group_sibling(g, k).start()
+
+    def group_last(g):
+        for k in range(2):
+            group_forward(g, k).wait_recv()
+        group_sibling(g, 2).start()
+
+    chunk_compute(0)
+
     group = tl // 128
 
     def combine(i):
@@ -485,57 +537,7 @@
         for _, to in proto_peers:
             feat_send(part, part, gs_s.at[0], gs_r.at[0], to)
 
-    span = 2 * CH
-    groups = pl_rows // span
-
-    def chunk_send(q, k):
-        to = (bat(1, 0), p) if k == 0 else (bat(nx - 1, 0), p)
-        part = gp_out.at[rows(b * pl_rows + q * CH, CH)]
-        return remote(part, part, out_s.at[0], g_r.at[k, q], to)
-
-    def group_forward(g, k):
-        block = bat(nx - 1, 0) if k == 0 else bat(1, 0)
-        to = (bat(1, 0), p) if k == 0 else (bat(nx - 1, 0), p)
-        part = gp_out.at[rows(block * pl_rows + g * span + k * CH, CH)]
-        return remote(part, part, out_s.at[0], f_r.at[k, g], to)
-
-    def group_sibling(g, k):
-        block = bat((nx - 1, 1, 2)[k], 0)
-        part = gp_out.at[rows(block * pl_rows + g * span, span)]
-        return remote(part, part, out_s.at[0], sib_r.at[0], sibling)
-
-    def own_sibling():
-        part = gp_out.at[rows(b * pl_rows, pl_rows)]
-        return remote(part, part, out_s.at[0], sib_r.at[0], sibling)
-
-    def chunk_compute(q):
-        sl = rows(q * CH, CH)
-        weight = ccol[sl, 0:1]
-        for j in range(tokens // 512):
-            js = slice(j * 512, (j + 1) * 512)
-            value = s[sl, js].astype(F32) * w_row[1, 0:1, js]
-            value = value - e[sl, js].astype(F32) * (w_row[0, 0:1, js] * weight)
-            delta[:, js] = value.astype(BF)
-        back = nn(delta[...], s_all[...])
-        unit, scale = unit_rows(sp[sl, :])
-        value = back_norm(back, unit, scale).astype(BF)
-        gp_out[rows(b * pl_rows + q * CH, CH), :] = value
-        chunk_send(q, 0).start()
-        chunk_send(q, 1).start()
-
-    def group_recv(g):
-        for k in range(2):
-            chunk_send(2 * g, k).wait_recv()
-            chunk_send(2 * g + 1, k).wait_recv()
-            group_forward(g, k).start()
-            group_sibling(g, k).start()
-
-    def group_last(g):
-        for k in range(2):
-            group_forward(g, k).wait_recv()
-        group_sibling(g, 2).start()
-
-    loop(chunks, chunk_compute)
+    loop(chunks - 1, lambda q: chunk_compute(q + 1))
     own_sibling().start()
     feat_middle()
     feat_x()

time: 105 us -> 102 us (0.971)
  Pallas kernels: 99.6 us -> 96.5 us
    pallas_call x1, Pallas kernels: 99.6 us -> 96.5 us  [on_device(): pl.pallas_call(functools.partial(kernel, nb, nq), out_shape=[pltpu.VMEM(s...]
where the time goes in v10:
time: 102 us; the launch traced here: 101 us
  Pallas kernels  96.5 us (95%)
  local copies, waits for them, and re-layouts  3.45 us (3%)
    pallas_call x1, Pallas kernels, on_device(): pl.pallas_call(functools.partial(kernel, nb, nq), out_shape=[pltpu.VMEM(s...  96.5 us
    unnamed x2, local copies, waits for them, and re-layouts  3.45 us

profile of v10, /device:TPU:0, one launch (start us, length us, event | category | flops | bytes accessed | tf_op | source)
XLA Modules:
  0.0 100.6 jit_solution(18244664675644370171)
XLA Ops:
  0.6 96.5 %prototype_head.1 = (bf16[8192,384]{1,0:T(8,128)(2,1)S(1)}, bf16[512,384]{1,0:T(8,128)(2,1)S(1)}) custom-call(bf16[512,384]{1,0:T(8,128)(2,1)} %sf_hbm.1, bf16[512,384]{1,0:T(8,128)(2,1)} %tf_hbm.1, bf16[8192,384]{1,0:T(8,128)(2,1)} %sp_hbm.1, bf16[8192,384]{1,0:T(8,128)(2,1)} %tp_hbm.1), custom_call_target="tpu_custom_call" | custom-call | tf_op jit(solution)/shard_map/prototype_head/pallas_call | solution.py:625
  97.1 2.7 %copy.8 = bf16[8192,384]{1,0:T(8,128)(2,1)} copy(bf16[8192,384]{1,0:T(8,128)(2,1)S(1)} %get-tuple-element.2) | data formatting | bytes 12582912
  99.8 0.7 copy.9

commit v11 on v10

--- a/solution.py
+++ b/solution.py
@@ -231,6 +231,9 @@
     def teacher_block(block, width, first=False):
         exp_block(anchor, t_all, e, block, width, LOG2E / teacher_temp, col_acc, first)
 
+    def student_block(block, width):
+        exp_block(pu, s_all, s, block, width, LOG2E / student_temp, row_acc, False)
+
     def student_plane(dx):
         if dx == far_dx:
             forward(1, dx).wait_recv()
@@ -355,12 +358,16 @@
     reduce_start(0)
     spread_start(1)
     student_plane(0)
+    near_part(1, 0)
     reduce_middle(0)
-    near_part(1, 0)
     near_part(1, 1)
+    for dx in near:
+        student_block(chip_block(dx) + c, tl)
     spread_end(1)
-    student_plane(near[0])
-    student_plane(near[1])
+    for dx in near:
+        for h in range(2):
+            near_forward(1, dx, h).wait_recv()
+        student_block(chip_block(dx) + 1 - c, tl)
     student_plane(far_dx)
     tokens_drain(0)
     weights = 1.0 / (tokens * reduce_end(0))
@@ -449,7 +456,7 @@
             group_forward(g, k).wait_recv()
         group_sibling(g, 2).start()
 
-    chunk_compute(0)
+    loop(2, chunk_compute)
 
     group = tl // 128
 
@@ -537,7 +544,7 @@
         for _, to in proto_peers:
             feat_send(part, part, gs_s.at[0], gs_r.at[0], to)
 
-    loop(chunks - 1, lambda q: chunk_compute(q + 1))
+    loop(chunks - 2, lambda q: chunk_compute(q + 2))
     own_sibling().start()
     feat_middle()
     feat_x()

time: 102 us -> 101 us (level)
  no operation moved by 1% of the time
where the time goes in v11:
time: 101 us; the launch traced here: 99.8 us
  Pallas kernels  95.7 us (95%)
  local copies, waits for them, and re-layouts  3.45 us (3%)
    pallas_call x1, Pallas kernels, on_device(): pl.pallas_call(functools.partial(kernel, nb, nq), out_shape=[pltpu.VMEM(s...  95.7 us
    unnamed x2, local copies, waits for them, and re-layouts  3.45 us

profile of v11, /device:TPU:0, one launch (start us, length us, event | category | flops | bytes accessed | tf_op | source)
XLA Modules:
  0.0 99.8 jit_solution(2782769640126601803)
XLA Ops:
  0.6 95.7 %prototype_head.1 = (bf16[8192,384]{1,0:T(8,128)(2,1)S(1)}, bf16[512,384]{1,0:T(8,128)(2,1)S(1)}) custom-call(bf16[512,384]{1,0:T(8,128)(2,1)} %sf_hbm.1, bf16[512,384]{1,0:T(8,128)(2,1)} %tf_hbm.1, bf16[8192,384]{1,0:T(8,128)(2,1)} %sp_hbm.1, bf16[8192,384]{1,0:T(8,128)(2,1)} %tp_hbm.1), custom_call_target="tpu_custom_call" | custom-call | tf_op jit(solution)/shard_map/prototype_head/pallas_call | solution.py:632
  96.4 2.7 %copy.8 = bf16[8192,384]{1,0:T(8,128)(2,1)} copy(bf16[8192,384]{1,0:T(8,128)(2,1)S(1)} %get-tuple-element.2) | data formatting | bytes 12582912
  99.1 0.7 copy.9
